TPU v7x, 128 devices: a whole 4x4x4 slice. The times are simulated.
128 devices in a mesh: tour: 64 (over y, z_lo, x, core), feat: 2 (over z_hi).
Axes of the slice: x: 4, y: 4, z: 4 (z_hi: 2, z_lo: 2; z = z_hi * 2 + z_lo), core: 2. Of those that a mesh axis runs over, the one named last changes fastest.
Arguments:
- projected: bfloat16 [32768, 1024], P('tour', 'feat'), may hold values from -220 to 220
- sharpness: float32 [], replicated, may hold values from 5 to 250
- partners: int32 [8, 64], replicated, may hold values from 0 to 63, as said below
- positives: int32 [32768], P('tour'), may hold values from 0 to 32767, as said below
Outputs:
- row_loss: float32 [32768], P('tour')
- view_grad: float32 [32768, 1024], P('tour', 'feat')
Inputs may be any that keep to these rules, and one draw needn't show every extreme that they name: For each round r there is one number m_r with partners[r, a] = a XOR m_r for every block a; m_r = M XOR s_r, where M is a nonzero multiple of 8 and s_0, ..., s_7 is an ordering of 0 to 7. positives pairs the views of each block of 512 views among themselves: positives_i lies in i's block, differs from i, and positives of positives_i is i.
All inputs are finite; a program needn't handle non-finite values.
Results may differ from a plain program's by a relative error of at most 0.008.
Values may be sent and summed in bfloat16 or wider, within the bound.
No kernel may reach another device: no remote copies, remote signals or barrier semaphores. Data moves between devices by JAX's collectives and lax.ppermute only.
A program may use at most 128 MiB of HBM per device.

v0:
```python
import functools

import jax
import jax.numpy as jnp
from jax import lax
from jax.experimental import pallas as pl
from jax.experimental.pallas import tpu as pltpu
from jax.sharding import PartitionSpec as P

EPSILON = 1e-06
ROWS = 512
HALF = 256
PIECE = 128
WIDTH = 1024
FEAT = 1
CORE = 2
X = {0: 0, 1: 4, 2: 8, 3: 12}
VMEM_BYTES = 24 * 1024 * 1024
F32 = jnp.float32
BF16 = jnp.bfloat16


def swap(value, mask):
    count = lax.axis_size(("tour", "feat"))
    pairs = [(source, source ^ mask) for source in range(count)]
    return lax.ppermute(value, ("tour", "feat"), pairs)


def spec(space=pltpu.VMEM):
    return pl.BlockSpec(memory_space=space)


def call(body, out_shape, smem, vmem, scratch=(), nflops=1):
    return pl.pallas_call(
        body,
        out_shape=out_shape,
        in_specs=[spec(pltpu.SMEM)] * len(smem) + [spec()] * len(vmem),
        out_specs=jax.tree.map(lambda _: spec(), out_shape),
        scratch_shapes=list(scratch),
        compiler_params=pltpu.CompilerParams(vmem_limit_bytes=VMEM_BYTES),
        cost_estimate=pl.CostEstimate(flops=nflops, bytes_accessed=1, transcendentals=0),
    )(*smem, *vmem)


def f32(*shape):
    return jax.ShapeDtypeStruct(shape, F32)


def bf16(*shape):
    return jax.ShapeDtypeStruct(shape, BF16)


def row_inverse(left, right):
    total = jnp.sum(left * left + right * right, -1, keepdims=True)
    return lax.rsqrt(total + EPSILON)


def embed_rows(left_ref, right_ref, out_ref, step=128):
    width = left_ref.shape[1]

    def chunk(index, carry):
        rows = pl.ds(pl.multiple_of(index * step, step), step)
        left = left_ref[rows, :].astype(F32)
        right = right_ref[rows, :].astype(F32)
        inverse = row_inverse(left, right)
        out_ref[rows, :width] = (left * inverse).astype(BF16)
        out_ref[rows, width:] = (right * inverse).astype(BF16)
        return carry

    lax.fori_loop(0, left_ref.shape[0] // step, chunk, 0)


def to_lanes(column):
    return jnp.broadcast_to(column, (128, 128)).T[0:1, :]


def to_rows(lanes):
    return jnp.broadcast_to(lanes, (128, 128)).T


def log_add(values):
    peak = functools.reduce(jnp.maximum, values)
    return peak + jnp.log(functools.reduce(jnp.add, [jnp.exp(value - peak) for value in values]))


def products(queries, keys):
    return lax.dot_general(queries, keys, (((1,), (1,)), ((), ())), preferred_element_type=F32)


def column_lse(score_ref, peak):
    total = jnp.zeros((8, score_ref.shape[1]), F32)
    for start in range(0, ROWS, 128):
        part = jnp.exp(score_ref[pl.ds(start, 128), :] - peak)
        total = total + jnp.sum(part.reshape(16, 8, part.shape[1]), axis=0)
    return peak + jnp.log(jnp.sum(total, axis=0, keepdims=True))


def column_peak(score_ref):
    peak = jnp.max(score_ref[pl.ds(0, 128), :], axis=0, keepdims=True)
    for start in range(128, ROWS, 128):
        peak = jnp.maximum(peak, jnp.max(score_ref[pl.ds(start, 128), :], axis=0, keepdims=True))
    return peak


def prep_kernel(half_ref, partner_ref, whole_ref, group_ref, near_ref, far_ref, met_ref, sems):
    half = half_ref[0]
    copies = [
        pltpu.make_async_copy(whole_ref.at[pl.ds(pl.multiple_of(part * HALF, HALF), HALF), :], out_ref, sems.at[j])
        for j, (part, out_ref) in enumerate(((half, near_ref), (1 - half, far_ref)))
    ]
    copies.append(pltpu.make_async_copy(partner_ref, met_ref, sems.at[2]))
    for copy in copies:
        copy.start()
    for copy in copies:
        copy.wait()
    group_ref[0] = jnp.right_shift(met_ref[0, 0], 3) - 1


def key_kernel(left_ref, right_ref, out_ref):
    for start in range(0, HALF, 128):
        rows = pl.ds(start, 128)
        embed_rows(left_ref.at[rows], right_ref.at[rows], out_ref.at[rows])


def own_kernel(
    half_ref, block_ref, sharp_ref, left_ref, right_ref, pos_ref, emb_ref, score_ref, lse_ref, hit_ref
):
    half = half_ref[0]
    embed_rows(left_ref, right_ref, emb_ref)
    mine = pl.ds(pl.multiple_of(half * HALF, HALF), HALF)
    score_ref[...] = products(emb_ref[...], emb_ref[mine, :]) * sharp_ref[0]
    columns = lax.broadcasted_iota(jnp.int32, (128, HALF), 1) + half * HALF
    rows = lax.broadcasted_iota(jnp.int32, (128, HALF), 0)
    pos = pos_ref[0:1, mine] - block_ref[0]
    hits = jnp.zeros((1, HALF), F32)
    for start in range(0, ROWS, 128):
        chunk = pl.ds(start, 128)
        part = score_ref[chunk, :]
        hits = hits + jnp.sum(jnp.where(rows + start == pos, part, 0.0), axis=0, keepdims=True)
        score_ref[chunk, :] = jnp.where(rows + start == columns, -jnp.inf, part)
    lse_ref[...] = column_lse(score_ref, column_peak(score_ref))
    hit_ref[...] = hits


def joined(refs):
    return refs[0][...] if len(refs) == 1 else jnp.concatenate([ref[...] for ref in refs], axis=0)


def tiles_kernel(sharp_ref, emb_ref, *refs):
    score_ref, row_ref, column_ref = refs[-3:]
    count = score_ref.shape[0]
    each = (len(refs) - 3) // count
    for j in range(count):
        score_ref[j] = products(emb_ref[...], joined(refs[j * each : (j + 1) * each])) * sharp_ref[0]
    for j in range(count):
        tile = score_ref.at[j]
        column_ref[j : j + 1, :] = column_lse(tile, column_peak(tile))
    for start in range(0, ROWS, 128):
        chunk = pl.ds(start, 128)
        slabs = [(j, pl.ds(k, 128)) for j in range(count) for k in (0, 128)]
        peak = functools.reduce(jnp.maximum, [score_ref[j, chunk, k] for j, k in slabs])
        peak = jnp.max(peak, axis=1, keepdims=True)
        total = functools.reduce(jnp.add, [jnp.exp(score_ref[j, chunk, k] - peak) for j, k in slabs])
        total = jnp.sum(total, axis=1, keepdims=True)
        row_ref[:, start : start + 128] = to_lanes(peak + jnp.log(total))


GROUPS = (0, 1, 3, 2)


def lse_kernel(sent_ref, back_ref, lse_ref, loss_ref):
    lse_ref[...] = log_add([sent_ref[0:1, :], back_ref[0:1, :]])
    loss_ref[...] = lse_ref[...] - (sent_ref[1:2, :] + back_ref[1:2, :])


def grad_kernel(start, *refs):
    half_ref, block_ref, sharp_ref, lse_ref = refs[:4]
    column_ref, left_ref, right_ref, pos_ref, own_ref, emb_ref = refs[4:10]
    score_refs = [ref.at[j] for ref in refs[10:13] for j in range(2)] + [ref.at[0] for ref in refs[13:15]]
    key_refs = [refs[15 + j : 16 + j] for j in range(6)] + [refs[21:23], refs[23:25]]
    near_ref, far_ref, weight_ref = refs[25:]
    half = half_ref[0]
    rows_count = near_ref.shape[0]
    mine = pl.ds(pl.multiple_of(half * HALF, HALF), HALF)
    own_lse = lse_ref[0:1, mine]
    pos = pos_ref[0:1, mine] - block_ref[0]
    for offset in range(0, rows_count, 128):
        chunk = pl.ds(start + offset, 128)
        out = pl.ds(offset, 128)
        base = to_rows(lse_ref[0:1, start + offset : start + offset + 128])
        base = jnp.concatenate([base, base], axis=1)
        rows = lax.broadcasted_iota(jnp.int32, (128, HALF), 0) + (start + offset)
        part = own_ref[chunk, :]
        weight = jnp.exp(part - base) + jnp.exp(part - own_lse) - jnp.where(rows == pos, 2.0, 0.0)
        weight_ref[out, 0:HALF] = weight.astype(BF16)
        for g in range(4):
            for core in range(2):
                tile = 1 + 2 * g + core
                part = score_refs[2 * g + core][chunk, :]
                column = column_ref[core : core + 1, g * HALF : (g + 1) * HALF]
                weight = jnp.exp(part - base) + jnp.exp(part - column)
                weight_ref[out, tile * HALF : (tile + 1) * HALF] = weight.astype(BF16)
    total = jnp.dot(weight_ref[:, 0:HALF], emb_ref[mine, :], preferred_element_type=F32)
    for tile in range(8):
        key = joined(key_refs[tile])
        total = total + jnp.dot(
            weight_ref[:, (tile + 1) * HALF : (tile + 2) * HALF], key, preferred_element_type=F32
        )
    total = total * sharp_ref[0]
    chunk = pl.ds(start, rows_count)
    left = left_ref[chunk, :].astype(F32)
    right = right_ref[chunk, :].astype(F32)
    inverse = row_inverse(left, right)
    width = left.shape[1]
    left, right = left * inverse, right * inverse
    near, far = total[:, :width], total[:, width:]
    radial = jnp.sum(left * near + right * far, -1, keepdims=True)
    near_ref[...] = inverse * (near - left * radial)
    far_ref[...] = (inverse * (far - right * radial)).astype(BF16)


def by_group(group, body, *values):
    return lax.switch(group, [functools.partial(body, 16 * bits) for bits in range(1, 8)], *values)


def swap_keys(mask, near, far):
    return swap(near, mask), swap(far, mask | FEAT)


def after(value, *done):
    return lax.optimization_barrier((value, *done))[0]


def shifted(columns, offset):
    at = [GROUPS.index(group ^ offset) * HALF for group in GROUPS]
    return jnp.concatenate([columns[:, start : start + HALF] for start in at], axis=1)


def per_device(projected, sharpness, partners, positives):
    half = lax.axis_index("feat").astype(jnp.int32)
    block = (lax.axis_index("tour") * ROWS).astype(jnp.int32)
    place = (half.reshape(1), block.reshape(1))
    sharp = sharpness.reshape(1)
    pos = positives.reshape(1, ROWS)
    other = swap(projected, FEAT)
    group, near_rows, far_rows = pl.pallas_call(
        prep_kernel,
        out_shape=(jax.ShapeDtypeStruct((1,), jnp.int32), bf16(HALF, WIDTH // 2), bf16(HALF, WIDTH // 2)),
        in_specs=[spec(pltpu.SMEM), spec(pl.ANY), spec(pl.ANY)],
        out_specs=(spec(pltpu.SMEM), spec(), spec()),
        scratch_shapes=[pltpu.SMEM((8, 64), jnp.int32), pltpu.SemaphoreType.DMA((3,))],
    )(place[0], partners, projected)
    first = call(key_kernel, bf16(HALF, WIDTH), (), by_group(group[0], swap_keys, near_rows, far_rows))
    held = {0: [first], 1: [swap(first, X[1])], 3: [swap(first, X[3])]}
    over, tiled = {0: [swap(first, CORE)]}, {}
    emb, own_scores, own_column, own_hit = call(
        own_kernel,
        (bf16(ROWS, WIDTH), f32(ROWS, HALF), f32(1, HALF), f32(1, HALF)),
        (*place, sharp),
        (projected, other, pos),
    )
    way = group[0] + 1
    met_column = own_column
    for along_y in (1, 2, 3):
        arrived = swap(own_column, 32 * along_y)
        met_column = jnp.where(jnp.right_shift(way, 1) == along_y, arrived, met_column)

    def tiles(*parts):
        count = len(parts)
        return call(
            tiles_kernel,
            (f32(count, ROWS, HALF), f32(1, ROWS), f32(count, HALF)),
            (sharp,),
            (emb, *[value for part in parts for value in part]),
        )

    tiled[0] = tiles(held[0], over[0])
    held[1], held[3], met_column = lax.optimization_barrier((held[1], held[3], met_column))
    met_column = jnp.where(jnp.bitwise_and(way, 1) == 1, swap(met_column, 16), met_column)
    held[2] = [swap(held[1][0][:PIECE], X[3]), swap(held[3][0][PIECE:], X[1])]
    for near in (1, 3):
        over[near] = [swap(held[near][0], CORE)]
        tiled[near] = tiles(held[near], over[near])
    held[2], tiled[0], tiled[1], tiled[3], met_column = lax.optimization_barrier(
        (held[2], tiled[0], tiled[1], tiled[3], met_column)
    )
    over[2] = [swap(piece, CORE) for piece in held[2]]
    tiled = [tiled[0], tiled[1], tiled[3], tiles(held[2]), tiles(over[2])]

    row_part = log_add([t[1] for t in tiled])
    spread = jnp.concatenate([own_column, own_column], axis=1)
    here = (lax.broadcasted_iota(jnp.int32, (1, ROWS), 1) // HALF) == half
    row_part = jnp.where(here, log_add([row_part, spread]), row_part)
    hits = jnp.where(here, jnp.concatenate([own_hit, own_hit], axis=1), 0.0)
    sent = jnp.concatenate([row_part, hits], axis=0)
    back = swap(sent, FEAT)
    lse, loss = call(lse_kernel, (f32(1, ROWS), f32(1, ROWS)), (), (sent, back), nflops=16_000_000_000)

    mine = jnp.concatenate([log_add([tiled[0][2][0:1], met_column])] + [t[2][0:1] for t in tiled[1:4]], axis=1)
    others = jnp.concatenate([t[2][1:2] for t in tiled[:3]] + [tiled[4][2]], axis=1)
    arrived = swap(jnp.concatenate([others, mine], axis=0), CORE)
    column = log_add([jnp.concatenate([mine, others], axis=0), arrived])
    for offset in (1, 3):
        if offset == 3:
            column = after(column, lse)
        column = log_add([column, shifted(swap(column, X[offset]), offset)])

    keys = [value for near in GROUPS for source in (held, over) for value in source[near]]
    near, far = [], []
    for start in (0, HALF):
        out = call(
            functools.partial(grad_kernel, start),
            (f32(HALF, WIDTH // 2), bf16(HALF, WIDTH // 2)),
            (*place, sharp),
            (lse, column, projected, other, pos, own_scores, emb, *[t[0] for t in tiled], *keys),
            scratch=[pltpu.VMEM((HALF, 9 * HALF), BF16)],
        )
        near.append(out[0])
        far.append(swap(out[1], FEAT))
    view_grad = jnp.concatenate([a + b.astype(F32) for a, b in zip(near, far, strict=True)], axis=0)
    return loss.reshape(ROWS), view_grad


def solution(mesh):
    in_specs = (P("tour", "feat"), P(), P(), P("tour"))
    out_specs = (P("tour"), P("tour", "feat"))
    return jax.shard_map(
        per_device, mesh=mesh, in_specs=in_specs, out_specs=out_specs, check_vma=False
    )
```

profile of v0, /device:TPU:0, one launch (start us, length us, event | category | flops | bytes accessed | tf_op | source)
XLA Modules:
  0.0 81.2 jit_solution(9201124216175085306)
XLA Ops:
  0.6 4.0 %collective-permute-start.16 = (bf16[512,512]{1,0:T(8,128)(2,1)}, bf16[512,512]{1,0:T(8,128)(2,1)S(1)}, u32[]{:S(2)}, u32[]{:S(2)}) collective-permute-start(bf16[512,512]{1,0:T(8,128)(2,1)} %refs_5_.3), channel_id=1, source_target_pairs={{0,1},{1,0},{2,3},{3,2},{4,5},{5,4},{6,7},{7,6},{8,9},{9,8},{10,11... | collective-permute-start | bytes 1572872 | tf_op jit(solution)/shard_map/ppermute | solution.py:26
  4.7 1.6 %shard_map.59 = (s32[1]{0:T(128)}, bf16[256,512]{1,0:T(8,128)(2,1)S(1)}, bf16[256,512]{1,0:T(8,128)(2,1)S(1)}) custom-call(s32[1]{0:T(128)} %bitcast.half_ref.refs_0_, s32[8,64]{1,0:T(8,128)} %partner_ref.1, bf16[512,512]{1,0:T(8,128)(2,1)} %refs_5_.3), custom_call_target="tpu_custom_call" | custom-call | tf_op jit(solution)/shard_map/pallas_call | solution.py:246
  6.9 14.7 %conditional.1 = (bf16[256,512]{1,0:T(8,128)(2,1)}, bf16[256,512]{1,0:T(8,128)(2,1)}) conditional(s32[]{:T(128)} %bitcast.1, (bf16[256,512]{1,0:T(8,128)(2,1)S(1)}, bf16[256,512]{1,0:T(8,128)(2,1)S(1)}) %tuple.39, (bf16[256,512]{1,0:T(8,128)(2,1)S(1)}, bf16[256,512]{1,0:T(8,128)(2,1)S(1)}) %tuple.39, ...), branch_computations={%region_0.0_spmd, %region_1.0_spmd, %region_2.0_spmd, %region_3.0_... | conditional | bytes 2097248 | solution.py:223
  6.9 3.1 %collective-permute-start.10 = (bf16[256,512]{1,0:T(8,128)(2,1)S(1)}, bf16[256,512]{1,0:T(8,128)(2,1)}, u32[]{:S(2)}, u32[]{:S(2)}) collective-permute-start(bf16[256,512]{1,0:T(8,128)(2,1)S(1)} %get-tuple-element.38), channel_id=1, source_target_pairs={{0,96},{1,97},{2,98},{3,99},{4,100},{5,101},{6,102},{7,103},{8,104... | collective-permute-start | bytes 786440 | tf_op jit(solution)/shard_map/cond/branch_5_fun/ppermute | solution.py:26
  10.0 0.0 collective-permute-start.11
  10.0 7.5 %collective-permute-done.10 = bf16[256,512]{1,0:T(8,128)(2,1)} collective-permute-done((bf16[256,512]{1,0:T(8,128)(2,1)S(1)}, bf16[256,512]{1,0:T(8,128)(2,1)}, u32[]{:S(2)}, u32[]{:S(2)}) %collective-permute-start.10) | collective-permute-done | bytes 262176 | tf_op jit(solution)/shard_map/cond/branch_5_fun/ppermute | solution.py:26
  17.6 4.1 %collective-permute-done.11 = bf16[256,512]{1,0:T(8,128)(2,1)} collective-permute-done((bf16[256,512]{1,0:T(8,128)(2,1)S(1)}, bf16[256,512]{1,0:T(8,128)(2,1)}, u32[]{:S(2)}, u32[]{:S(2)}) %collective-permute-start.11) | collective-permute-done | bytes 262176 | tf_op jit(solution)/shard_map/cond/branch_5_fun/ppermute | solution.py:26
  21.6 1.3 %shard_map.60.refs_0_.refs_15_ = bf16[256,1024]{1,0:T(8,128)(2,1)S(1)} custom-call(bf16[256,512]{1,0:T(8,128)(2,1)} %get-tuple-element.93.left_ref, bf16[256,512]{1,0:T(8,128)(2,1)} %get-tuple-element.94.right_ref), custom_call_target="tpu_custom_call" | custom-call | flops 1 | bytes 1 | tf_op jit(solution)/shard_map/pallas_call | solution.py:34
  22.9 1.6 %collective-permute-start.14 = (bf16[256,1024]{1,0:T(8,128)(2,1)S(1)}, bf16[256,1024]{1,0:T(8,128)(2,1)S(1)}, u32[]{:S(2)}, u32[]{:S(2)}) collective-permute-start(bf16[256,1024]{1,0:T(8,128)(2,1)S(1)} %shard_map.60.refs_0_.refs_15_), channel_id=1, source_target_pairs={{0,4},{1,5},{2,6},{3,7},{4,0},{5,1},{6,2},{7,3},{8,12},{9,13},{10,... | collective-permute-start | bytes 1572872 | tf_op jit(solution)/shard_map/ppermute | solution.py:26
  24.5 2.1 %collective-permute-start.15 = (bf16[256,1024]{1,0:T(8,128)(2,1)S(1)}, bf16[256,1024]{1,0:T(8,128)(2,1)S(1)}, u32[]{:S(2)}, u32[]{:S(2)}) collective-permute-start(bf16[256,1024]{1,0:T(8,128)(2,1)S(1)} %shard_map.60.refs_0_.refs_15_), channel_id=1, source_target_pairs={{0,12},{1,13},{2,14},{3,15},{4,8},{5,9},{6,10},{7,11},{8,4},{9,5},... | collective-permute-start | bytes 1572872 | tf_op jit(solution)/shard_map/ppermute | solution.py:26
  26.6 0.0 collective-permute-start.22
  27.2 0.0 collective-permute-done.16.right_ref.refs_6_
  27.2 0.0 copy-start.1
  27.2 0.0 copy-done
  27.3 0.7 copy-done.1
  27.9 1.1 %shard_map.61 = (bf16[512,1024]{1,0:T(8,128)(2,1)S(1)}, f32[512,256]{1,0:T(8,128)S(1)}, f32[1,256]{1,0:T(1,128)S(1)}, f32[1,256]{1,0:T(1,128)S(1)}) custom-call(s32[1]{0:T(128)} %bitcast.half_ref.refs_0_, s32[1]{0:T(128)} %bitcast.3.block_ref.refs_1_, f32[1]{0:T(128)} %bitcast.10.sharp_ref, bf16[512,512]{1,0:T(8,128)(2,1)S(1)} %copy-done, ...), custom_call_target="tpu_custom_call" | custom-call | flops 1 | bytes 1 | tf_op jit(solution)/shard_map/pallas_call | solution.py:34
  29.1 3.0 %collective-permute-start.17 = (f32[1,256]{1,0:T(1,128)S(1)}, f32[1,256]{1,0:T(1,128)S(1)}, u32[]{:S(2)}, u32[]{:S(2)}) collective-permute-start(f32[1,256]{1,0:T(1,128)S(1)} %get-tuple-element.95), channel_id=1, source_target_pairs={{0,96},{1,97},{2,98},{3,99},{4,100},{5,101},{6,102},{7,103},{8,104... | collective-permute-start | bytes 3080 | tf_op jit(solution)/shard_map/ppermute | solution.py:26
  32.1 0.0 collective-permute-start.18
  32.1 1.8 %collective-permute-done.17 = f32[1,256]{1,0:T(1,128)S(1)} collective-permute-done((f32[1,256]{1,0:T(1,128)S(1)}, f32[1,256]{1,0:T(1,128)S(1)}, u32[]{:S(2)}, u32[]{:S(2)}) %collective-permute-start.17) | collective-permute-done | bytes 1056 | tf_op jit(solution)/shard_map/ppermute | solution.py:26
  33.9 0.0 collective-permute-start.19
  34.6 2.6 %collective-permute-done.18 = f32[1,256]{1,0:T(1,128)S(1)} collective-permute-done((f32[1,256]{1,0:T(1,128)S(1)}, f32[1,256]{1,0:T(1,128)S(1)}, u32[]{:S(2)}, u32[]{:S(2)}) %collective-permute-start.18) | collective-permute-done | bytes 1056 | tf_op jit(solution)/shard_map/ppermute | solution.py:26
  37.2 0.3 collective-permute-done.19
  37.5 0.0 collective-permute-done.14.refs_0_.refs_17_
  37.5 0.3 collective-permute-done.15.refs_0_.refs_19_
  37.8 0.0 collective-permute-start.23
  37.8 0.5 collective-permute-start.24
  38.3 0.0 collective-permute-done.22.refs_1_.refs_16_
  38.3 1.1 %shard_map.62 = (f32[2,512,256]{2,1,0:T(8,128)S(1)}, f32[1,512]{1,0:T(1,128)S(1)}, f32[2,256]{1,0:T(2,128)S(1)}) custom-call(f32[1]{0:T(128)} %bitcast.11.sharp_ref, bf16[512,1024]{1,0:T(8,128)(2,1)S(1)} %get-tuple-element.98.emb_ref.refs_9_, bf16[256,1024]{1,0:T(8,128)(2,1)S(1)} %shard_map.60.refs_0_.refs_15_, ...), custom_call_target="tpu_custom_call" | custom-call | flops 1 | bytes 1 | tf_op jit(solution)/shard_map/pallas_call | solution.py:34
  39.5 2.2 %collective-permute-start.20 = (bf16[128,1024]{1,0:T(8,128)(2,1)S(1)}, bf16[128,1024]{1,0:T(8,128)(2,1)S(1)}, u32[]{:S(2)}, u32[]{:S(2)}) collective-permute-start(bf16[128,1024]{1,0:T(8,128)(2,1)S(1)} %slice.46), channel_id=1, source_target_pairs={{0,12},{1,13},{2,14},{3,15},{4,8},{5,9},{6,10},{7,11},{8,4},{9,5},... | collective-permute-start | bytes 786440 | tf_op jit(solution)/shard_map/ppermute | solution.py:26
  41.7 0.0 collective-permute-start.21
  41.7 1.5 %collective-permute-start.25 = (f32[1,256]{1,0:T(1,128)S(1)}, f32[1,256]{1,0:T(1,128)S(1)}, u32[]{:S(2)}, u32[]{:S(2)}) collective-permute-start(f32[1,256]{1,0:T(1,128)S(1)} %get-tuple-element.108), channel_id=1, source_target_pairs={{0,16},{1,17},{2,18},{3,19},{4,20},{5,21},{6,22},{7,23},{8,24},{9,... | collective-permute-start | bytes 3080 | tf_op jit(solution)/shard_map/ppermute | solution.py:26
  43.2 2.0 %collective-permute-done.25 = f32[1,256]{1,0:T(1,128)S(1)} collective-permute-done((f32[1,256]{1,0:T(1,128)S(1)}, f32[1,256]{1,0:T(1,128)S(1)}, u32[]{:S(2)}, u32[]{:S(2)}) %collective-permute-start.25) | collective-permute-done | bytes 1056 | tf_op jit(solution)/shard_map/ppermute | solution.py:26
  45.2 0.0 collective-permute-done.23.refs_1_.refs_18_
  45.2 1.1 %shard_map.63 = (f32[2,512,256]{2,1,0:T(8,128)S(1)}, f32[1,512]{1,0:T(1,128)S(1)}, f32[2,256]{1,0:T(2,128)S(1)}) custom-call(f32[1]{0:T(128)} %bitcast.12.sharp_ref, bf16[512,1024]{1,0:T(8,128)(2,1)S(1)} %get-tuple-element.98.emb_ref.refs_9_, bf16[256,1024]{1,0:T(8,128)(2,1)S(1)} %collective-permute-done.14.refs_0_.refs_17_, ...), custom_call_target="tpu_custom_call" | custom-call | flops 1 | bytes 1 | tf_op jit(solution)/shard_map/pallas_call | solution.py:34
  46.3 0.0 collective-permute-done.24.refs_1_.refs_20_
  46.3 1.1 %shard_map.64 = (f32[2,512,256]{2,1,0:T(8,128)S(1)}, f32[1,512]{1,0:T(1,128)S(1)}, f32[2,256]{1,0:T(2,128)S(1)}) custom-call(f32[1]{0:T(128)} %bitcast.13.sharp_ref, bf16[512,1024]{1,0:T(8,128)(2,1)S(1)} %get-tuple-element.98.emb_ref.refs_9_, bf16[256,1024]{1,0:T(8,128)(2,1)S(1)} %collective-permute-done.15.refs_0_.refs_19_, ...), custom_call_target="tpu_custom_call" | custom-call | flops 1 | bytes 1 | tf_op jit(solution)/shard_map/pallas_call | solution.py:34
  47.4 1.6 %collective-permute-done.20.refs_0_.refs_21_ = bf16[128,1024]{1,0:T(8,128)(2,1)S(1)} collective-permute-done((bf16[128,1024]{1,0:T(8,128)(2,1)S(1)}, bf16[128,1024]{1,0:T(8,128)(2,1)S(1)}, u32[]{:S(2)}, u32[]{:S(2)}) %collective-permute-start.20) | collective-permute-done | bytes 262176 | tf_op jit(solution)/shard_map/ppermute | solution.py:26
  49.0 0.6 collective-permute-done.21.refs_1_.refs_22_
  49.6 0.0 collective-permute-start.26
  49.6 0.5 collective-permute-start.27
  50.1 0.7 shard_map.65
  50.8 0.3 collective-permute-done.26.refs_0_.refs_23_
  51.1 0.4 collective-permute-done.27.refs_1_.refs_24_
  51.5 0.7 shard_map.66
  52.2 0.2 collective-permute-start.29
  52.4 0.1 compare_select_fusion.1
  52.5 3.4 %collective-permute-start.28 = (f32[2,512]{1,0:T(2,128)S(1)}, f32[2,512]{1,0:T(2,128)S(1)}, u32[]{:S(2)}, u32[]{:S(2)}) collective-permute-start(f32[2,512]{1,0:T(2,128)S(1)} %pad_maximum_fusion.3.sent_ref), channel_id=1, source_target_pairs={{0,1},{1,0},{2,3},{3,2},{4,5},{5,4},{6,7},{7,6},{8,9},{9,8},{10,11... | collective-permute-start | bytes 12296 | tf_op jit(solution)/shard_map/ppermute | solution.py:26
  55.9 0.0 collective-permute-done.29
  56.0 0.4 collective-permute-start.30
  56.3 1.4 %collective-permute-done.28.back_ref = f32[2,512]{1,0:T(2,128)S(1)} collective-permute-done((f32[2,512]{1,0:T(2,128)S(1)}, f32[2,512]{1,0:T(2,128)S(1)}, u32[]{:S(2)}, u32[]{:S(2)}) %collective-permute-start.28) | collective-permute-done | bytes 4128 | tf_op jit(solution)/shard_map/ppermute | solution.py:26
  57.7 0.6 shard_map.67
  58.3 1.4 %collective-permute-done.30 = f32[2,1024]{1,0:T(2,128)S(1)} collective-permute-done((f32[2,1024]{1,0:T(2,128)S(1)}, f32[2,1024]{1,0:T(2,128)S(1)}, u32[]{:S(2)}, u32[]{:S(2)}) %collective-permute-start.30) | collective-permute-done | bytes 8224 | tf_op jit(solution)/shard_map/ppermute | solution.py:26
  59.7 0.1 log_add_fusion.1
  59.7 1.6 %collective-permute-start.31 = (f32[2,1024]{1,0:T(2,128)S(1)}, f32[2,1024]{1,0:T(2,128)S(1)}, u32[]{:S(2)}, u32[]{:S(2)}) collective-permute-start(f32[2,1024]{1,0:T(2,128)S(1)} %log_add_fusion.1), channel_id=1, source_target_pairs={{0,12},{1,13},{2,14},{3,15},{4,8},{5,9},{6,10},{7,11},{8,4},{9,5},... | collective-permute-start | bytes 24584 | tf_op jit(solution)/shard_map/ppermute | solution.py:26
  61.3 3.4 %collective-permute-done.31 = f32[2,1024]{1,0:T(2,128)S(1)} collective-permute-done((f32[2,1024]{1,0:T(2,128)S(1)}, f32[2,1024]{1,0:T(2,128)S(1)}, u32[]{:S(2)}, u32[]{:S(2)}) %collective-permute-start.31) | collective-permute-done | bytes 8224 | tf_op jit(solution)/shard_map/ppermute | solution.py:26
  64.7 1.7 %shard_map.69 = (f32[256,512]{1,0:T(8,128)S(1)}, bf16[256,512]{1,0:T(8,128)(2,1)S(1)}) custom-call(s32[1]{0:T(128)} %bitcast.half_ref.refs_0_, s32[1]{0:T(128)} %bitcast.3.block_ref.refs_1_, f32[1]{0:T(128)} %bitcast.17.refs_2_, f32[1,512]{1,0:T(1,128)S(1)} %get-tuple-element.118.refs_3_, f32[2,1024]{1,0:T(2,128)S(1)} %log_add_fusion.refs_4_, ...), custom_call_target="tpu_custom_call" | custom-call | flops 1 | bytes 1 | tf_op jit(solution)/shard_map/pallas_call | solution.py:34
  66.5 2.0 %collective-permute-start.33 = (bf16[256,512]{1,0:T(8,128)(2,1)S(1)}, bf16[256,512]{1,0:T(8,128)(2,1)S(1)}, u32[]{:S(2)}, u32[]{:S(2)}) collective-permute-start(bf16[256,512]{1,0:T(8,128)(2,1)S(1)} %get-tuple-element.135), channel_id=1, source_target_pairs={{0,1},{1,0},{2,3},{3,2},{4,5},{5,4},{6,7},{7,6},{8,9},{9,8},{10,11... | collective-permute-start | bytes 786440 | tf_op jit(solution)/shard_map/ppermute | solution.py:26
  68.5 1.7 %shard_map.68 = (f32[256,512]{1,0:T(8,128)S(1)}, bf16[256,512]{1,0:T(8,128)(2,1)S(1)}) custom-call(s32[1]{0:T(128)} %bitcast.half_ref.refs_0_, s32[1]{0:T(128)} %bitcast.3.block_ref.refs_1_, f32[1]{0:T(128)} %bitcast.16.refs_2_, f32[1,512]{1,0:T(1,128)S(1)} %get-tuple-element.118.refs_3_, f32[2,1024]{1,0:T(2,128)S(1)} %log_add_fusion.refs_4_, ...), custom_call_target="tpu_custom_call" | custom-call | flops 1 | bytes 1 | tf_op jit(solution)/shard_map/pallas_call | solution.py:34
  70.2 1.7 %collective-permute-start.32 = (bf16[256,512]{1,0:T(8,128)(2,1)S(1)}, bf16[256,512]{1,0:T(8,128)(2,1)S(1)}, u32[]{:S(2)}, u32[]{:S(2)}) collective-permute-start(bf16[256,512]{1,0:T(8,128)(2,1)S(1)} %get-tuple-element.133), channel_id=1, source_target_pairs={{0,1},{1,0},{2,3},{3,2},{4,5},{5,4},{6,7},{7,6},{8,9},{9,8},{10,11... | collective-permute-start | bytes 786440 | tf_op jit(solution)/shard_map/ppermute | solution.py:26
  71.9 4.9 %collective-permute-done.33 = bf16[256,512]{1,0:T(8,128)(2,1)S(1)} collective-permute-done((bf16[256,512]{1,0:T(8,128)(2,1)S(1)}, bf16[256,512]{1,0:T(8,128)(2,1)S(1)}, u32[]{:S(2)}, u32[]{:S(2)}) %collective-permute-start.33) | collective-permute-done | bytes 262176 | tf_op jit(solution)/shard_map/ppermute | solution.py:26
  76.8 0.1 convert_add_fusion
  76.8 3.2 %collective-permute-done.32 = bf16[256,512]{1,0:T(8,128)(2,1)S(1)} collective-permute-done((bf16[256,512]{1,0:T(8,128)(2,1)S(1)}, bf16[256,512]{1,0:T(8,128)(2,1)S(1)}, u32[]{:S(2)}, u32[]{:S(2)}) %collective-permute-start.32) | collective-permute-done | bytes 262176 | tf_op jit(solution)/shard_map/ppermute | solution.py:26
  80.0 0.1 convert_add_fusion.1
  80.1 1.0 %pad_maximum_fusion = f32[512,512]{1,0:T(8,128)} fusion(f32[256,512]{1,0:T(8,128)S(1)} %convert_add_fusion, f32[256,512]{1,0:T(8,128)S(1)} %convert_add_fusion.1), kind=kLoop, calls=%fused_computation | loop fusion | flops 262144 | bytes 2097152 | tf_op jit(solution)/shard_map/concatenate | solution.py:320
  (15 shorter events, 0.2 us)
Async XLA Ops:
  0.6 26.6 %collective-permute-start.16 = (bf16[512,512]{1,0:T(8,128)(2,1)}, bf16[512,512]{1,0:T(8,128)(2,1)S(1)}, u32[]{:S(2)}, u32[]{:S(2)}) collective-permute-start(bf16[512,512]{1,0:T(8,128)(2,1)} %refs_5_.3), channel_id=1, source_target_pairs={{0,1},{1,0},{2,3},{3,2},{4,5},{5,4},{6,7},{7,6},{8,9},{9,8},{10,11... | collective-permute-start | bytes 1572872 | tf_op jit(solution)/shard_map/ppermute | solution.py:26
  6.9 10.6 %collective-permute-start.10 = (bf16[256,512]{1,0:T(8,128)(2,1)S(1)}, bf16[256,512]{1,0:T(8,128)(2,1)}, u32[]{:S(2)}, u32[]{:S(2)}) collective-permute-start(bf16[256,512]{1,0:T(8,128)(2,1)S(1)} %get-tuple-element.38), channel_id=1, source_target_pairs={{0,96},{1,97},{2,98},{3,99},{4,100},{5,101},{6,102},{7,103},{8,104... | collective-permute-start | bytes 786440 | tf_op jit(solution)/shard_map/cond/branch_5_fun/ppermute | solution.py:26
  10.0 11.6 %collective-permute-start.11 = (bf16[256,512]{1,0:T(8,128)(2,1)S(1)}, bf16[256,512]{1,0:T(8,128)(2,1)}, u32[]{:S(2)}, u32[]{:S(2)}) collective-permute-start(bf16[256,512]{1,0:T(8,128)(2,1)S(1)} %get-tuple-element.39), channel_id=1, source_target_pairs={{0,97},{1,96},{2,99},{3,98},{4,101},{5,100},{6,103},{7,102},{8,105... | collective-permute-start | bytes 786440 | tf_op jit(solution)/shard_map/cond/branch_5_fun/ppermute | solution.py:26
  21.6 5.6 %copy-start = (bf16[512,512]{1,0:T(8,128)(2,1)S(1)}, bf16[512,512]{1,0:T(8,128)(2,1)}, u32[]{:S(2)}) copy-start(bf16[512,512]{1,0:T(8,128)(2,1)} %refs_5_.3) | copy-start | bytes 1572868
  22.9 14.6 %collective-permute-start.14 = (bf16[256,1024]{1,0:T(8,128)(2,1)S(1)}, bf16[256,1024]{1,0:T(8,128)(2,1)S(1)}, u32[]{:S(2)}, u32[]{:S(2)}) collective-permute-start(bf16[256,1024]{1,0:T(8,128)(2,1)S(1)} %shard_map.60.refs_0_.refs_15_), channel_id=1, source_target_pairs={{0,4},{1,5},{2,6},{3,7},{4,0},{5,1},{6,2},{7,3},{8,12},{9,13},{10,... | collective-permute-start | bytes 1572872 | tf_op jit(solution)/shard_map/ppermute | solution.py:26
  24.5 13.3 %collective-permute-start.15 = (bf16[256,1024]{1,0:T(8,128)(2,1)S(1)}, bf16[256,1024]{1,0:T(8,128)(2,1)S(1)}, u32[]{:S(2)}, u32[]{:S(2)}) collective-permute-start(bf16[256,1024]{1,0:T(8,128)(2,1)S(1)} %shard_map.60.refs_0_.refs_15_), channel_id=1, source_target_pairs={{0,12},{1,13},{2,14},{3,15},{4,8},{5,9},{6,10},{7,11},{8,4},{9,5},... | collective-permute-start | bytes 1572872 | tf_op jit(solution)/shard_map/ppermute | solution.py:26
  26.6 11.8 %collective-permute-start.22 = (bf16[256,1024]{1,0:T(8,128)(2,1)S(1)}, bf16[256,1024]{1,0:T(8,128)(2,1)S(1)}, u32[]{:S(2)}, u32[]{:S(2)}) collective-permute-start(bf16[256,1024]{1,0:T(8,128)(2,1)S(1)} %shard_map.60.refs_0_.refs_15_), channel_id=1, source_target_pairs={{0,2},{1,3},{2,0},{3,1},{4,6},{5,7},{6,4},{7,5},{8,10},{9,11},{10,... | collective-permute-start | bytes 1572872 | tf_op jit(solution)/shard_map/ppermute | solution.py:26
  27.2 0.7 copy-start.1
  29.1 4.9 %collective-permute-start.17 = (f32[1,256]{1,0:T(1,128)S(1)}, f32[1,256]{1,0:T(1,128)S(1)}, u32[]{:S(2)}, u32[]{:S(2)}) collective-permute-start(f32[1,256]{1,0:T(1,128)S(1)} %get-tuple-element.95), channel_id=1, source_target_pairs={{0,96},{1,97},{2,98},{3,99},{4,100},{5,101},{6,102},{7,103},{8,104... | collective-permute-start | bytes 3080 | tf_op jit(solution)/shard_map/ppermute | solution.py:26
  32.1 5.1 %collective-permute-start.18 = (f32[1,256]{1,0:T(1,128)S(1)}, f32[1,256]{1,0:T(1,128)S(1)}, u32[]{:S(2)}, u32[]{:S(2)}) collective-permute-start(f32[1,256]{1,0:T(1,128)S(1)} %get-tuple-element.95), channel_id=1, source_target_pairs={{0,64},{1,65},{2,66},{3,67},{4,68},{5,69},{6,70},{7,71},{8,72},{9,... | collective-permute-start | bytes 3080 | tf_op jit(solution)/shard_map/ppermute | solution.py:26
  33.9 3.6 %collective-permute-start.19 = (f32[1,256]{1,0:T(1,128)S(1)}, f32[1,256]{1,0:T(1,128)S(1)}, u32[]{:S(2)}, u32[]{:S(2)}) collective-permute-start(f32[1,256]{1,0:T(1,128)S(1)} %get-tuple-element.95), channel_id=1, source_target_pairs={{0,32},{1,33},{2,34},{3,35},{4,36},{5,37},{6,38},{7,39},{8,40},{9,... | collective-permute-start | bytes 3080 | tf_op jit(solution)/shard_map/ppermute | solution.py:26
  37.8 7.4 %collective-permute-start.23 = (bf16[256,1024]{1,0:T(8,128)(2,1)S(1)}, bf16[256,1024]{1,0:T(8,128)(2,1)S(1)}, u32[]{:S(2)}, u32[]{:S(2)}) collective-permute-start(bf16[256,1024]{1,0:T(8,128)(2,1)S(1)} %collective-permute-done.14.refs_0_.refs_17_), channel_id=1, source_target_pairs={{0,2},{1,3},{2,0},{3,1},{4,6},{5,7},{6,4},{7,5},{8,10},{9,11},{10,... | collective-permute-start | bytes 1572872 | tf_op jit(solution)/shard_map/ppermute | solution.py:26
  37.8 8.5 %collective-permute-start.24 = (bf16[256,1024]{1,0:T(8,128)(2,1)S(1)}, bf16[256,1024]{1,0:T(8,128)(2,1)S(1)}, u32[]{:S(2)}, u32[]{:S(2)}) collective-permute-start(bf16[256,1024]{1,0:T(8,128)(2,1)S(1)} %collective-permute-done.15.refs_0_.refs_19_), channel_id=1, source_target_pairs={{0,2},{1,3},{2,0},{3,1},{4,6},{5,7},{6,4},{7,5},{8,10},{9,11},{10,... | collective-permute-start | bytes 1572872 | tf_op jit(solution)/shard_map/ppermute | solution.py:26
  39.5 9.5 %collective-permute-start.20 = (bf16[128,1024]{1,0:T(8,128)(2,1)S(1)}, bf16[128,1024]{1,0:T(8,128)(2,1)S(1)}, u32[]{:S(2)}, u32[]{:S(2)}) collective-permute-start(bf16[128,1024]{1,0:T(8,128)(2,1)S(1)} %slice.46), channel_id=1, source_target_pairs={{0,12},{1,13},{2,14},{3,15},{4,8},{5,9},{6,10},{7,11},{8,4},{9,5},... | collective-permute-start | bytes 786440 | tf_op jit(solution)/shard_map/ppermute | solution.py:26
  41.7 7.9 %collective-permute-start.21 = (bf16[128,1024]{1,0:T(8,128)(2,1)S(1)}, bf16[128,1024]{1,0:T(8,128)(2,1)S(1)}, u32[]{:S(2)}, u32[]{:S(2)}) collective-permute-start(bf16[128,1024]{1,0:T(8,128)(2,1)S(1)} %slice.47), channel_id=1, source_target_pairs={{0,4},{1,5},{2,6},{3,7},{4,0},{5,1},{6,2},{7,3},{8,12},{9,13},{10,... | collective-permute-start | bytes 786440 | tf_op jit(solution)/shard_map/ppermute | solution.py:26
  41.7 3.6 %collective-permute-start.25 = (f32[1,256]{1,0:T(1,128)S(1)}, f32[1,256]{1,0:T(1,128)S(1)}, u32[]{:S(2)}, u32[]{:S(2)}) collective-permute-start(f32[1,256]{1,0:T(1,128)S(1)} %get-tuple-element.108), channel_id=1, source_target_pairs={{0,16},{1,17},{2,18},{3,19},{4,20},{5,21},{6,22},{7,23},{8,24},{9,... | collective-permute-start | bytes 3080 | tf_op jit(solution)/shard_map/ppermute | solution.py:26
  49.6 1.5 %collective-permute-start.26 = (bf16[128,1024]{1,0:T(8,128)(2,1)S(1)}, bf16[128,1024]{1,0:T(8,128)(2,1)S(1)}, u32[]{:S(2)}, u32[]{:S(2)}) collective-permute-start(bf16[128,1024]{1,0:T(8,128)(2,1)S(1)} %collective-permute-done.20.refs_0_.refs_21_), channel_id=1, source_target_pairs={{0,2},{1,3},{2,0},{3,1},{4,6},{5,7},{6,4},{7,5},{8,10},{9,11},{10,... | collective-permute-start | bytes 786440 | tf_op jit(solution)/shard_map/ppermute | solution.py:26
  49.6 1.9 %collective-permute-start.27 = (bf16[128,1024]{1,0:T(8,128)(2,1)S(1)}, bf16[128,1024]{1,0:T(8,128)(2,1)S(1)}, u32[]{:S(2)}, u32[]{:S(2)}) collective-permute-start(bf16[128,1024]{1,0:T(8,128)(2,1)S(1)} %collective-permute-done.21.refs_1_.refs_22_), channel_id=1, source_target_pairs={{0,2},{1,3},{2,0},{3,1},{4,6},{5,7},{6,4},{7,5},{8,10},{9,11},{10,... | collective-permute-start | bytes 786440 | tf_op jit(solution)/shard_map/ppermute | solution.py:26
  52.2 3.7 %collective-permute-start.29 = (f32[2,1024]{1,0:T(2,128)S(1)}, f32[2,1024]{1,0:T(2,128)S(1)}, u32[]{:S(2)}, u32[]{:S(2)}) collective-permute-start(f32[2,1024]{1,0:T(2,128)S(1)} %maximum_maximum_fusion.1), channel_id=1, source_target_pairs={{0,2},{1,3},{2,0},{3,1},{4,6},{5,7},{6,4},{7,5},{8,10},{9,11},{10,... | collective-permute-start | bytes 24584 | tf_op jit(solution)/shard_map/ppermute | solution.py:26
  52.5 5.2 %collective-permute-start.28 = (f32[2,512]{1,0:T(2,128)S(1)}, f32[2,512]{1,0:T(2,128)S(1)}, u32[]{:S(2)}, u32[]{:S(2)}) collective-permute-start(f32[2,512]{1,0:T(2,128)S(1)} %pad_maximum_fusion.3.sent_ref), channel_id=1, source_target_pairs={{0,1},{1,0},{2,3},{3,2},{4,5},{5,4},{6,7},{7,6},{8,9},{9,8},{10,11... | collective-permute-start | bytes 12296 | tf_op jit(solution)/shard_map/ppermute | solution.py:26
  56.0 3.7 %collective-permute-start.30 = (f32[2,1024]{1,0:T(2,128)S(1)}, f32[2,1024]{1,0:T(2,128)S(1)}, u32[]{:S(2)}, u32[]{:S(2)}) collective-permute-start(f32[2,1024]{1,0:T(2,128)S(1)} %log_add_fusion.2), channel_id=1, source_target_pairs={{0,4},{1,5},{2,6},{3,7},{4,0},{5,1},{6,2},{7,3},{8,12},{9,13},{10,... | collective-permute-start | bytes 24584 | tf_op jit(solution)/shard_map/ppermute | solution.py:26
  59.7 4.9 %collective-permute-start.31 = (f32[2,1024]{1,0:T(2,128)S(1)}, f32[2,1024]{1,0:T(2,128)S(1)}, u32[]{:S(2)}, u32[]{:S(2)}) collective-permute-start(f32[2,1024]{1,0:T(2,128)S(1)} %log_add_fusion.1), channel_id=1, source_target_pairs={{0,12},{1,13},{2,14},{3,15},{4,8},{5,9},{6,10},{7,11},{8,4},{9,5},... | collective-permute-start | bytes 24584 | tf_op jit(solution)/shard_map/ppermute | solution.py:26
  66.5 10.3 %collective-permute-start.33 = (bf16[256,512]{1,0:T(8,128)(2,1)S(1)}, bf16[256,512]{1,0:T(8,128)(2,1)S(1)}, u32[]{:S(2)}, u32[]{:S(2)}) collective-permute-start(bf16[256,512]{1,0:T(8,128)(2,1)S(1)} %get-tuple-element.135), channel_id=1, source_target_pairs={{0,1},{1,0},{2,3},{3,2},{4,5},{5,4},{6,7},{7,6},{8,9},{9,8},{10,11... | collective-permute-start | bytes 786440 | tf_op jit(solution)/shard_map/ppermute | solution.py:26
  70.2 9.8 %collective-permute-start.32 = (bf16[256,512]{1,0:T(8,128)(2,1)S(1)}, bf16[256,512]{1,0:T(8,128)(2,1)S(1)}, u32[]{:S(2)}, u32[]{:S(2)}) collective-permute-start(bf16[256,512]{1,0:T(8,128)(2,1)S(1)} %get-tuple-element.133), channel_id=1, source_target_pairs={{0,1},{1,0},{2,3},{3,2},{4,5},{5,4},{6,7},{7,6},{8,9},{9,8},{10,11... | collective-permute-start | bytes 786440 | tf_op jit(solution)/shard_map/ppermute | solution.py:26
where the time goes:
time: 82.3 us; the launch traced here: 81.2 us
  waiting for transfers between devices  35.8 us (43%)
  starting transfers between devices  27.8 us (34%)
  Pallas kernels  12.7 us (15%)
  between operations  2.75 us (3%)
  other arithmetic  1.44 us (2%)
    ppermute x22, waiting for transfers between devices, swap(): return lax.ppermute(value, ('tour', 'feat'), pairs)  35.8 us
    ppermute x22, starting transfers between devices, swap(): return lax.ppermute(value, ('tour', 'feat'), pairs)  27.8 us
    pallas_call x10, Pallas kernels, call(): pl.pallas_call(body, out_shape=out_shape, in_specs=[spec(pltpu.SMEM)] * l...  11.1 us
  transfers between devices with their start and end apart: 22, of which 16 were waited for; matrix products, arithmetic and copies ran while one was open for 0% of the time, Pallas kernels for 13%

commit v1 on v0

--- a/solution.py
+++ b/solution.py
@@ -116,10 +116,17 @@
     group_ref[0] = jnp.right_shift(met_ref[0, 0], 3) - 1
 
 
-def key_kernel(left_ref, right_ref, out_ref):
-    for start in range(0, HALF, 128):
-        rows = pl.ds(start, 128)
-        embed_rows(left_ref.at[rows], right_ref.at[rows], out_ref.at[rows])
+def key_kernel(left_ref, right_ref, out_ref, *piece_refs):
+    width = left_ref.shape[1]
+    for start, piece_ref in zip((0, PIECE), piece_refs, strict=True):
+        rows = pl.ds(start, PIECE)
+        left = left_ref[rows, :].astype(F32)
+        right = right_ref[rows, :].astype(F32)
+        inverse = row_inverse(left, right)
+        for half, columns in ((left, slice(0, width)), (right, slice(width, 2 * width))):
+            embedded = (half * inverse).astype(BF16)
+            out_ref[rows, columns] = embedded
+            piece_ref[:, columns] = embedded
 
 
 def own_kernel(
@@ -149,9 +156,12 @@
 def tiles_kernel(sharp_ref, emb_ref, *refs):
     score_ref, row_ref, column_ref = refs[-3:]
     count = score_ref.shape[0]
-    each = (len(refs) - 3) // count
+    keys = list(refs[:-3])
     for j in range(count):
-        score_ref[j] = products(emb_ref[...], joined(refs[j * each : (j + 1) * each])) * sharp_ref[0]
+        part = [keys.pop(0)]
+        if part[0].shape[0] == PIECE:
+            part.append(keys.pop(0))
+        score_ref[j] = products(emb_ref[...], joined(part)) * sharp_ref[0]
     for j in range(count):
         tile = score_ref.at[j]
         column_ref[j : j + 1, :] = column_lse(tile, column_peak(tile))
@@ -177,8 +187,12 @@
     half_ref, block_ref, sharp_ref, lse_ref = refs[:4]
     column_ref, left_ref, right_ref, pos_ref, own_ref, emb_ref = refs[4:10]
     score_refs = [ref.at[j] for ref in refs[10:13] for j in range(2)] + [ref.at[0] for ref in refs[13:15]]
-    key_refs = [refs[15 + j : 16 + j] for j in range(6)] + [refs[21:23], refs[23:25]]
-    near_ref, far_ref, weight_ref = refs[25:]
+    keys, key_refs = list(refs[15:-3]), []
+    while keys:
+        count = HALF // keys[0].shape[0]
+        key_refs.append(keys[:count])
+        keys = keys[count:]
+    near_ref, far_ref, weight_ref = refs[-3:]
     half = half_ref[0]
     rows_count = near_ref.shape[0]
     mine = pl.ds(pl.multiple_of(half * HALF, HALF), HALF)
@@ -250,9 +264,10 @@
         out_specs=(spec(pltpu.SMEM), spec(), spec()),
         scratch_shapes=[pltpu.SMEM((8, 64), jnp.int32), pltpu.SemaphoreType.DMA((3,))],
     )(place[0], partners, projected)
-    first = call(key_kernel, bf16(HALF, WIDTH), (), by_group(group[0], swap_keys, near_rows, far_rows))
+    piece = bf16(PIECE, WIDTH)
+    first, *pieces = call(key_kernel, (bf16(HALF, WIDTH), piece, piece), (), by_group(group[0], swap_keys, near_rows, far_rows))
     held = {0: [first], 1: [swap(first, X[1])], 3: [swap(first, X[3])]}
-    over, tiled = {0: [swap(first, CORE)]}, {}
+    over, tiled = {0: [swap(piece, CORE) for piece in pieces]}, {}
     emb, own_scores, own_column, own_hit = call(
         own_kernel,
         (bf16(ROWS, WIDTH), f32(ROWS, HALF), f32(1, HALF), f32(1, HALF)),
@@ -275,15 +290,13 @@
         )
 
     tiled[0] = tiles(held[0], over[0])
-    held[1], held[3], met_column = lax.optimization_barrier((held[1], held[3], met_column))
+    held[1], held[3], met_column, tiled[0] = lax.optimization_barrier((held[1], held[3], met_column, tiled[0]))
     met_column = jnp.where(jnp.bitwise_and(way, 1) == 1, swap(met_column, 16), met_column)
     held[2] = [swap(held[1][0][:PIECE], X[3]), swap(held[3][0][PIECE:], X[1])]
     for near in (1, 3):
         over[near] = [swap(held[near][0], CORE)]
         tiled[near] = tiles(held[near], over[near])
-    held[2], tiled[0], tiled[1], tiled[3], met_column = lax.optimization_barrier(
-        (held[2], tiled[0], tiled[1], tiled[3], met_column)
-    )
+    held[2], tiled[1], tiled[3], met_column = lax.optimization_barrier((held[2], tiled[1], tiled[3], met_column))
     over[2] = [swap(piece, CORE) for piece in held[2]]
     tiled = [tiled[0], tiled[1], tiled[3], tiles(held[2]), tiles(over[2])]
 
@@ -294,15 +307,13 @@
     hits = jnp.where(here, jnp.concatenate([own_hit, own_hit], axis=1), 0.0)
     sent = jnp.concatenate([row_part, hits], axis=0)
     back = swap(sent, FEAT)
-    lse, loss = call(lse_kernel, (f32(1, ROWS), f32(1, ROWS)), (), (sent, back), nflops=16_000_000_000)
+    lse, loss = call(lse_kernel, (f32(1, ROWS), f32(1, ROWS)), (), (sent, back), nflops=2_500_000_000)
 
     mine = jnp.concatenate([log_add([tiled[0][2][0:1], met_column])] + [t[2][0:1] for t in tiled[1:4]], axis=1)
     others = jnp.concatenate([t[2][1:2] for t in tiled[:3]] + [tiled[4][2]], axis=1)
     arrived = swap(jnp.concatenate([others, mine], axis=0), CORE)
     column = log_add([jnp.concatenate([mine, others], axis=0), arrived])
     for offset in (1, 3):
-        if offset == 3:
-            column = after(column, lse)
         column = log_add([column, shifted(swap(column, X[offset]), offset)])
 
     keys = [value for near in GROUPS for source in (held, over) for value in source[near]]

time: 82.3 us -> 79.9 us (0.971)
  waiting for transfers between devices: 35.8 us -> 30.9 us
  starting transfers between devices: 27.8 us -> 29.3 us
    ppermute x22 -> x23, waiting for transfers between devices: 35.8 us -> 30.9 us  [swap(): return lax.ppermute(value, ('tour', 'feat'), pairs)]
    ppermute x22 -> x23, starting transfers between devices: 27.8 us -> 29.3 us  [swap(): return lax.ppermute(value, ('tour', 'feat'), pairs)]
  transfers between devices with their start and end apart: 22 -> 23, of which waited for: 16 -> 14; matrix products, arithmetic and copies ran while one was open for 0% -> 0% of each run, Pallas kernels for 13% -> 14%
where the time goes in v1:
time: 79.9 us; the launch traced here: 78.6 us
  waiting for transfers between devices  30.9 us (39%)
  starting transfers between devices  29.3 us (37%)
  Pallas kernels  13.4 us (17%)
  between operations  2.76 us (3%)
  other arithmetic  1.43 us (2%)
    ppermute x23, waiting for transfers between devices, swap(): return lax.ppermute(value, ('tour', 'feat'), pairs)  30.9 us
    ppermute x23, starting transfers between devices, swap(): return lax.ppermute(value, ('tour', 'feat'), pairs)  29.3 us
    pallas_call x10, Pallas kernels, call(): pl.pallas_call(body, out_shape=out_shape, in_specs=[spec(pltpu.SMEM)] * l...  11.7 us
    pallas_call x1, Pallas kernels, per_device(): pl.pallas_call(prep_kernel, out_shape=(jax.ShapeDtypeStruct((1,), jnp.int...  1.64 us
  transfers between devices with their start and end apart: 23, of which 14 were waited for; matrix products, arithmetic and copies ran while one was open for 0% of the time, Pallas kernels for 14%

profile of v1, /device:TPU:0, one launch (start us, length us, event | category | flops | bytes accessed | tf_op | source)
XLA Modules:
  0.0 78.6 jit_solution(6988189153925457719)
XLA Ops:
  0.6 4.0 %collective-permute-start.16 = (bf16[512,512]{1,0:T(8,128)(2,1)}, bf16[512,512]{1,0:T(8,128)(2,1)S(1)}, u32[]{:S(2)}, u32[]{:S(2)}) collective-permute-start(bf16[512,512]{1,0:T(8,128)(2,1)} %refs_5_.3), channel_id=1, source_target_pairs={{0,1},{1,0},{2,3},{3,2},{4,5},{5,4},{6,7},{7,6},{8,9},{9,8},{10,11... | collective-permute-start | bytes 1572872 | tf_op jit(solution)/shard_map/ppermute | solution.py:26
  4.7 1.6 %shard_map.59 = (s32[1]{0:T(128)}, bf16[256,512]{1,0:T(8,128)(2,1)S(1)}, bf16[256,512]{1,0:T(8,128)(2,1)S(1)}) custom-call(s32[1]{0:T(128)} %bitcast.half_ref.refs_0_, s32[8,64]{1,0:T(8,128)} %partner_ref.1, bf16[512,512]{1,0:T(8,128)(2,1)} %refs_5_.3), custom_call_target="tpu_custom_call" | custom-call | tf_op jit(solution)/shard_map/pallas_call | solution.py:260
  7.0 14.7 %conditional.1 = (bf16[256,512]{1,0:T(8,128)(2,1)}, bf16[256,512]{1,0:T(8,128)(2,1)}) conditional(s32[]{:T(128)} %bitcast.1, (bf16[256,512]{1,0:T(8,128)(2,1)S(1)}, bf16[256,512]{1,0:T(8,128)(2,1)S(1)}) %tuple.38, (bf16[256,512]{1,0:T(8,128)(2,1)S(1)}, bf16[256,512]{1,0:T(8,128)(2,1)S(1)}) %tuple.38, ...), branch_computations={%region_0.0_spmd, %region_1.0_spmd, %region_2.0_spmd, %region_3.0_... | conditional | bytes 2097248 | solution.py:237
  7.0 3.1 %collective-permute-start.10 = (bf16[256,512]{1,0:T(8,128)(2,1)S(1)}, bf16[256,512]{1,0:T(8,128)(2,1)}, u32[]{:S(2)}, u32[]{:S(2)}) collective-permute-start(bf16[256,512]{1,0:T(8,128)(2,1)S(1)} %get-tuple-element.38), channel_id=1, source_target_pairs={{0,96},{1,97},{2,98},{3,99},{4,100},{5,101},{6,102},{7,103},{8,104... | collective-permute-start | bytes 786440 | tf_op jit(solution)/shard_map/cond/branch_5_fun/ppermute | solution.py:26
  10.1 0.0 collective-permute-start.11
  10.1 7.5 %collective-permute-done.10 = bf16[256,512]{1,0:T(8,128)(2,1)} collective-permute-done((bf16[256,512]{1,0:T(8,128)(2,1)S(1)}, bf16[256,512]{1,0:T(8,128)(2,1)}, u32[]{:S(2)}, u32[]{:S(2)}) %collective-permute-start.10) | collective-permute-done | bytes 262176 | tf_op jit(solution)/shard_map/cond/branch_5_fun/ppermute | solution.py:26
  17.6 4.1 %collective-permute-done.11 = bf16[256,512]{1,0:T(8,128)(2,1)} collective-permute-done((bf16[256,512]{1,0:T(8,128)(2,1)S(1)}, bf16[256,512]{1,0:T(8,128)(2,1)}, u32[]{:S(2)}, u32[]{:S(2)}) %collective-permute-start.11) | collective-permute-done | bytes 262176 | tf_op jit(solution)/shard_map/cond/branch_5_fun/ppermute | solution.py:26
  21.7 1.9 %shard_map.60 = (bf16[256,1024]{1,0:T(8,128)(2,1)S(1)}, bf16[128,1024]{1,0:T(8,128)(2,1)}, bf16[128,1024]{1,0:T(8,128)(2,1)S(1)}) custom-call(bf16[256,512]{1,0:T(8,128)(2,1)} %get-tuple-element.95.left_ref, bf16[256,512]{1,0:T(8,128)(2,1)} %get-tuple-element.96.right_ref), custom_call_target="tpu_custom_call" | custom-call | flops 1 | bytes 1 | tf_op jit(solution)/shard_map/pallas_call | solution.py:34
  23.6 1.5 %collective-permute-start.14 = (bf16[256,1024]{1,0:T(8,128)(2,1)S(1)}, bf16[256,1024]{1,0:T(8,128)(2,1)S(1)}, u32[]{:S(2)}, u32[]{:S(2)}) collective-permute-start(bf16[256,1024]{1,0:T(8,128)(2,1)S(1)} %get-tuple-element.97.refs_0_.refs_15_), channel_id=1, source_target_pairs={{0,4},{1,5},{2,6},{3,7},{4,0},{5,1},{6,2},{7,3},{8,12},{9,13},{10,... | collective-permute-start | bytes 1572872 | tf_op jit(solution)/shard_map/ppermute | solution.py:26
  25.1 2.1 %collective-permute-start.15 = (bf16[256,1024]{1,0:T(8,128)(2,1)S(1)}, bf16[256,1024]{1,0:T(8,128)(2,1)S(1)}, u32[]{:S(2)}, u32[]{:S(2)}) collective-permute-start(bf16[256,1024]{1,0:T(8,128)(2,1)S(1)} %get-tuple-element.97.refs_0_.refs_15_), channel_id=1, source_target_pairs={{0,12},{1,13},{2,14},{3,15},{4,8},{5,9},{6,10},{7,11},{8,4},{9,5},... | collective-permute-start | bytes 1572872 | tf_op jit(solution)/shard_map/ppermute | solution.py:26
  27.1 0.0 collective-permute-start.20
  27.1 0.5 collective-permute-start.21
  28.3 0.0 collective-permute-done.16.right_ref.refs_6_
  28.3 0.0 copy-start.1
  28.3 0.7 copy-done.1
  29.0 1.1 %shard_map.61 = (bf16[512,1024]{1,0:T(8,128)(2,1)S(1)}, f32[512,256]{1,0:T(8,128)S(1)}, f32[1,256]{1,0:T(1,128)S(1)}, f32[1,256]{1,0:T(1,128)S(1)}) custom-call(s32[1]{0:T(128)} %bitcast.half_ref.refs_0_, s32[1]{0:T(128)} %bitcast.3.block_ref.refs_1_, f32[1]{0:T(128)} %bitcast.10.sharp_ref, bf16[512,512]{1,0:T(8,128)(2,1)S(1)} %copy-done, ...), custom_call_target="tpu_custom_call" | custom-call | flops 1 | bytes 1 | tf_op jit(solution)/shard_map/pallas_call | solution.py:34
  30.2 3.0 %collective-permute-start.17 = (f32[1,256]{1,0:T(1,128)S(1)}, f32[1,256]{1,0:T(1,128)S(1)}, u32[]{:S(2)}, u32[]{:S(2)}) collective-permute-start(f32[1,256]{1,0:T(1,128)S(1)} %get-tuple-element.98), channel_id=1, source_target_pairs={{0,96},{1,97},{2,98},{3,99},{4,100},{5,101},{6,102},{7,103},{8,104... | collective-permute-start | bytes 3080 | tf_op jit(solution)/shard_map/ppermute | solution.py:26
  33.2 0.0 collective-permute-done.20.refs_1_.refs_16_
  33.2 0.0 collective-permute-start.18
  33.2 0.0 collective-permute-done.21.refs_2_.refs_17_
  33.2 1.1 %collective-permute-start.19 = (f32[1,256]{1,0:T(1,128)S(1)}, f32[1,256]{1,0:T(1,128)S(1)}, u32[]{:S(2)}, u32[]{:S(2)}) collective-permute-start(f32[1,256]{1,0:T(1,128)S(1)} %get-tuple-element.98), channel_id=1, source_target_pairs={{0,32},{1,33},{2,34},{3,35},{4,36},{5,37},{6,38},{7,39},{8,40},{9,... | collective-permute-start | bytes 3080 | tf_op jit(solution)/shard_map/ppermute | solution.py:26
  35.0 1.1 %shard_map.62 = (f32[2,512,256]{2,1,0:T(8,128)S(1)}, f32[1,512]{1,0:T(1,128)S(1)}, f32[2,256]{1,0:T(2,128)S(1)}) custom-call(f32[1]{0:T(128)} %bitcast.11.sharp_ref, bf16[512,1024]{1,0:T(8,128)(2,1)S(1)} %get-tuple-element.99.emb_ref.refs_9_, bf16[256,1024]{1,0:T(8,128)(2,1)S(1)} %get-tuple-element.97.refs_0_.refs_15_, ...), custom_call_target="tpu_custom_call" | custom-call | flops 1 | bytes 1 | tf_op jit(solution)/shard_map/pallas_call | solution.py:34
  36.1 0.0 collective-permute-done.17
  36.1 2.2 %collective-permute-done.18 = f32[1,256]{1,0:T(1,128)S(1)} collective-permute-done((f32[1,256]{1,0:T(1,128)S(1)}, f32[1,256]{1,0:T(1,128)S(1)}, u32[]{:S(2)}, u32[]{:S(2)}) %collective-permute-start.18) | collective-permute-done | bytes 1056 | tf_op jit(solution)/shard_map/ppermute | solution.py:26
  38.3 0.0 collective-permute-done.19
  38.3 0.0 collective-permute-done.14.refs_0_.refs_18_
  38.3 0.1 collective-permute-done.15.refs_0_.refs_20_
  38.4 0.0 collective-permute-start.24
  38.4 0.5 collective-permute-start.25
  39.0 2.2 %collective-permute-start.22 = (bf16[128,1024]{1,0:T(8,128)(2,1)S(1)}, bf16[128,1024]{1,0:T(8,128)(2,1)S(1)}, u32[]{:S(2)}, u32[]{:S(2)}) collective-permute-start(bf16[128,1024]{1,0:T(8,128)(2,1)S(1)} %slice.46), channel_id=1, source_target_pairs={{0,12},{1,13},{2,14},{3,15},{4,8},{5,9},{6,10},{7,11},{8,4},{9,5},... | collective-permute-start | bytes 786440 | tf_op jit(solution)/shard_map/ppermute | solution.py:26
  41.1 0.0 collective-permute-start.23
  41.2 1.5 %collective-permute-start.26 = (f32[1,256]{1,0:T(1,128)S(1)}, f32[1,256]{1,0:T(1,128)S(1)}, u32[]{:S(2)}, u32[]{:S(2)}) collective-permute-start(f32[1,256]{1,0:T(1,128)S(1)} %get-tuple-element.114), channel_id=1, source_target_pairs={{0,16},{1,17},{2,18},{3,19},{4,20},{5,21},{6,22},{7,23},{8,24},{9,... | collective-permute-start | bytes 3080 | tf_op jit(solution)/shard_map/ppermute | solution.py:26
  42.7 2.1 %collective-permute-done.26 = f32[1,256]{1,0:T(1,128)S(1)} collective-permute-done((f32[1,256]{1,0:T(1,128)S(1)}, f32[1,256]{1,0:T(1,128)S(1)}, u32[]{:S(2)}, u32[]{:S(2)}) %collective-permute-start.26) | collective-permute-done | bytes 1056 | tf_op jit(solution)/shard_map/ppermute | solution.py:26
  44.7 0.0 collective-permute-done.24.refs_1_.refs_19_
  44.7 1.1 %shard_map.63 = (f32[2,512,256]{2,1,0:T(8,128)S(1)}, f32[1,512]{1,0:T(1,128)S(1)}, f32[2,256]{1,0:T(2,128)S(1)}) custom-call(f32[1]{0:T(128)} %bitcast.12.sharp_ref, bf16[512,1024]{1,0:T(8,128)(2,1)S(1)} %get-tuple-element.99.emb_ref.refs_9_, bf16[256,1024]{1,0:T(8,128)(2,1)S(1)} %collective-permute-done.14.refs_0_.refs_18_, ...), custom_call_target="tpu_custom_call" | custom-call | flops 1 | bytes 1 | tf_op jit(solution)/shard_map/pallas_call | solution.py:34
  45.8 0.0 collective-permute-done.25.refs_1_.refs_21_
  45.8 1.1 %shard_map.64 = (f32[2,512,256]{2,1,0:T(8,128)S(1)}, f32[1,512]{1,0:T(1,128)S(1)}, f32[2,256]{1,0:T(2,128)S(1)}) custom-call(f32[1]{0:T(128)} %bitcast.13.sharp_ref, bf16[512,1024]{1,0:T(8,128)(2,1)S(1)} %get-tuple-element.99.emb_ref.refs_9_, bf16[256,1024]{1,0:T(8,128)(2,1)S(1)} %collective-permute-done.15.refs_0_.refs_20_, ...), custom_call_target="tpu_custom_call" | custom-call | flops 1 | bytes 1 | tf_op jit(solution)/shard_map/pallas_call | solution.py:34
  46.9 1.6 %collective-permute-done.22.refs_0_.refs_22_ = bf16[128,1024]{1,0:T(8,128)(2,1)S(1)} collective-permute-done((bf16[128,1024]{1,0:T(8,128)(2,1)S(1)}, bf16[128,1024]{1,0:T(8,128)(2,1)S(1)}, u32[]{:S(2)}, u32[]{:S(2)}) %collective-permute-start.22) | collective-permute-done | bytes 262176 | tf_op jit(solution)/shard_map/ppermute | solution.py:26
  48.5 0.5 collective-permute-done.23.refs_1_.refs_23_
  49.1 0.0 collective-permute-start.27
  49.1 0.5 collective-permute-start.28
  49.6 0.7 shard_map.65
  50.3 0.3 collective-permute-done.27.refs_0_.refs_24_
  50.6 0.4 collective-permute-done.28.refs_1_.refs_25_
  51.0 0.7 shard_map.66
  51.7 0.2 collective-permute-start.30
  51.9 0.1 compare_select_fusion.1
  52.0 1.0 %collective-permute-done.30 = f32[2,1024]{1,0:T(2,128)S(1)} collective-permute-done((f32[2,1024]{1,0:T(2,128)S(1)}, f32[2,1024]{1,0:T(2,128)S(1)}, u32[]{:S(2)}, u32[]{:S(2)}) %collective-permute-start.30) | collective-permute-done | bytes 8224 | tf_op jit(solution)/shard_map/ppermute | solution.py:26
  53.0 0.4 collective-permute-start.31
  53.4 3.4 %collective-permute-start.29 = (f32[2,512]{1,0:T(2,128)S(1)}, f32[2,512]{1,0:T(2,128)S(1)}, u32[]{:S(2)}, u32[]{:S(2)}) collective-permute-start(f32[2,512]{1,0:T(2,128)S(1)} %pad_maximum_fusion.3.sent_ref), channel_id=1, source_target_pairs={{0,1},{1,0},{2,3},{3,2},{4,5},{5,4},{6,7},{7,6},{8,9},{9,8},{10,11... | collective-permute-start | bytes 12296 | tf_op jit(solution)/shard_map/ppermute | solution.py:26
  56.8 0.1 log_add_fusion.1
  56.8 1.6 %collective-permute-start.32 = (f32[2,1024]{1,0:T(2,128)S(1)}, f32[2,1024]{1,0:T(2,128)S(1)}, u32[]{:S(2)}, u32[]{:S(2)}) collective-permute-start(f32[2,1024]{1,0:T(2,128)S(1)} %log_add_fusion.1), channel_id=1, source_target_pairs={{0,12},{1,13},{2,14},{3,15},{4,8},{5,9},{6,10},{7,11},{8,4},{9,5},... | collective-permute-start | bytes 24584 | tf_op jit(solution)/shard_map/ppermute | solution.py:26
  58.4 0.2 collective-permute-done.29.back_ref
  58.6 0.6 shard_map.67
  59.2 2.6 %collective-permute-done.32 = f32[2,1024]{1,0:T(2,128)S(1)} collective-permute-done((f32[2,1024]{1,0:T(2,128)S(1)}, f32[2,1024]{1,0:T(2,128)S(1)}, u32[]{:S(2)}, u32[]{:S(2)}) %collective-permute-start.32) | collective-permute-done | bytes 8224 | tf_op jit(solution)/shard_map/ppermute | solution.py:26
  61.8 1.7 %shard_map.69 = (f32[256,512]{1,0:T(8,128)S(1)}, bf16[256,512]{1,0:T(8,128)(2,1)S(1)}) custom-call(s32[1]{0:T(128)} %bitcast.half_ref.refs_0_, s32[1]{0:T(128)} %bitcast.3.block_ref.refs_1_, f32[1]{0:T(128)} %bitcast.17.refs_2_, f32[1,512]{1,0:T(1,128)S(1)} %get-tuple-element.123.refs_3_, f32[2,1024]{1,0:T(2,128)S(1)} %log_add_fusion.refs_4_, ...), custom_call_target="tpu_custom_call" | custom-call | flops 1 | bytes 1 | tf_op jit(solution)/shard_map/pallas_call | solution.py:34
  63.5 3.4 %collective-permute-start.34 = (bf16[256,512]{1,0:T(8,128)(2,1)S(1)}, bf16[256,512]{1,0:T(8,128)(2,1)S(1)}, u32[]{:S(2)}, u32[]{:S(2)}) collective-permute-start(bf16[256,512]{1,0:T(8,128)(2,1)S(1)} %get-tuple-element.139), channel_id=1, source_target_pairs={{0,1},{1,0},{2,3},{3,2},{4,5},{5,4},{6,7},{7,6},{8,9},{9,8},{10,11... | collective-permute-start | bytes 786440 | tf_op jit(solution)/shard_map/ppermute | solution.py:26
  66.9 1.7 %shard_map.68 = (f32[256,512]{1,0:T(8,128)S(1)}, bf16[256,512]{1,0:T(8,128)(2,1)S(1)}) custom-call(s32[1]{0:T(128)} %bitcast.half_ref.refs_0_, s32[1]{0:T(128)} %bitcast.3.block_ref.refs_1_, f32[1]{0:T(128)} %bitcast.16.refs_2_, f32[1,512]{1,0:T(1,128)S(1)} %get-tuple-element.123.refs_3_, f32[2,1024]{1,0:T(2,128)S(1)} %log_add_fusion.refs_4_, ...), custom_call_target="tpu_custom_call" | custom-call | flops 1 | bytes 1 | tf_op jit(solution)/shard_map/pallas_call | solution.py:34
  68.6 0.3 collective-permute-start.33
  69.0 4.4 %collective-permute-done.34 = bf16[256,512]{1,0:T(8,128)(2,1)S(1)} collective-permute-done((bf16[256,512]{1,0:T(8,128)(2,1)S(1)}, bf16[256,512]{1,0:T(8,128)(2,1)S(1)}, u32[]{:S(2)}, u32[]{:S(2)}) %collective-permute-start.34) | collective-permute-done | bytes 262176 | tf_op jit(solution)/shard_map/ppermute | solution.py:26
  73.3 0.1 convert_add_fusion
  73.4 4.0 %collective-permute-done.33 = bf16[256,512]{1,0:T(8,128)(2,1)S(1)} collective-permute-done((bf16[256,512]{1,0:T(8,128)(2,1)S(1)}, bf16[256,512]{1,0:T(8,128)(2,1)S(1)}, u32[]{:S(2)}, u32[]{:S(2)}) %collective-permute-start.33) | collective-permute-done | bytes 262176 | tf_op jit(solution)/shard_map/ppermute | solution.py:26
  77.4 0.1 convert_add_fusion.1
  77.5 1.0 %pad_maximum_fusion = f32[512,512]{1,0:T(8,128)} fusion(f32[256,512]{1,0:T(8,128)S(1)} %convert_add_fusion, f32[256,512]{1,0:T(8,128)S(1)} %convert_add_fusion.1), kind=kLoop, calls=%fused_computation | loop fusion | flops 262144 | bytes 2097152 | tf_op jit(solution)/shard_map/concatenate | solution.py:331
  (17 shorter events, 0.2 us)
Async XLA Ops:
  0.6 27.7 %collective-permute-start.16 = (bf16[512,512]{1,0:T(8,128)(2,1)}, bf16[512,512]{1,0:T(8,128)(2,1)S(1)}, u32[]{:S(2)}, u32[]{:S(2)}) collective-permute-start(bf16[512,512]{1,0:T(8,128)(2,1)} %refs_5_.3), channel_id=1, source_target_pairs={{0,1},{1,0},{2,3},{3,2},{4,5},{5,4},{6,7},{7,6},{8,9},{9,8},{10,11... | collective-permute-start | bytes 1572872 | tf_op jit(solution)/shard_map/ppermute | solution.py:26
  4.7 23.7 %copy-start = (bf16[512,512]{1,0:T(8,128)(2,1)S(1)}, bf16[512,512]{1,0:T(8,128)(2,1)}, u32[]{:S(2)}) copy-start(bf16[512,512]{1,0:T(8,128)(2,1)} %refs_5_.3) | copy-start | bytes 1572868
  7.0 10.6 %collective-permute-start.10 = (bf16[256,512]{1,0:T(8,128)(2,1)S(1)}, bf16[256,512]{1,0:T(8,128)(2,1)}, u32[]{:S(2)}, u32[]{:S(2)}) collective-permute-start(bf16[256,512]{1,0:T(8,128)(2,1)S(1)} %get-tuple-element.38), channel_id=1, source_target_pairs={{0,96},{1,97},{2,98},{3,99},{4,100},{5,101},{6,102},{7,103},{8,104... | collective-permute-start | bytes 786440 | tf_op jit(solution)/shard_map/cond/branch_5_fun/ppermute | solution.py:26
  10.1 11.6 %collective-permute-start.11 = (bf16[256,512]{1,0:T(8,128)(2,1)S(1)}, bf16[256,512]{1,0:T(8,128)(2,1)}, u32[]{:S(2)}, u32[]{:S(2)}) collective-permute-start(bf16[256,512]{1,0:T(8,128)(2,1)S(1)} %get-tuple-element.39), channel_id=1, source_target_pairs={{0,97},{1,96},{2,99},{3,98},{4,101},{5,100},{6,103},{7,102},{8,105... | collective-permute-start | bytes 786440 | tf_op jit(solution)/shard_map/cond/branch_5_fun/ppermute | solution.py:26
  23.6 14.7 %collective-permute-start.14 = (bf16[256,1024]{1,0:T(8,128)(2,1)S(1)}, bf16[256,1024]{1,0:T(8,128)(2,1)S(1)}, u32[]{:S(2)}, u32[]{:S(2)}) collective-permute-start(bf16[256,1024]{1,0:T(8,128)(2,1)S(1)} %get-tuple-element.97.refs_0_.refs_15_), channel_id=1, source_target_pairs={{0,4},{1,5},{2,6},{3,7},{4,0},{5,1},{6,2},{7,3},{8,12},{9,13},{10,... | collective-permute-start | bytes 1572872 | tf_op jit(solution)/shard_map/ppermute | solution.py:26
  25.1 13.3 %collective-permute-start.15 = (bf16[256,1024]{1,0:T(8,128)(2,1)S(1)}, bf16[256,1024]{1,0:T(8,128)(2,1)S(1)}, u32[]{:S(2)}, u32[]{:S(2)}) collective-permute-start(bf16[256,1024]{1,0:T(8,128)(2,1)S(1)} %get-tuple-element.97.refs_0_.refs_15_), channel_id=1, source_target_pairs={{0,12},{1,13},{2,14},{3,15},{4,8},{5,9},{6,10},{7,11},{8,4},{9,5},... | collective-permute-start | bytes 1572872 | tf_op jit(solution)/shard_map/ppermute | solution.py:26
  27.1 6.0 %collective-permute-start.20 = (bf16[128,1024]{1,0:T(8,128)(2,1)}, bf16[128,1024]{1,0:T(8,128)(2,1)S(1)}, u32[]{:S(2)}, u32[]{:S(2)}) collective-permute-start(bf16[128,1024]{1,0:T(8,128)(2,1)} %get-tuple-element.100), channel_id=1, source_target_pairs={{0,2},{1,3},{2,0},{3,1},{4,6},{5,7},{6,4},{7,5},{8,10},{9,11},{10,... | collective-permute-start | bytes 786440 | tf_op jit(solution)/shard_map/ppermute | solution.py:26
  27.1 6.0 %collective-permute-start.21 = (bf16[128,1024]{1,0:T(8,128)(2,1)S(1)}, bf16[128,1024]{1,0:T(8,128)(2,1)S(1)}, u32[]{:S(2)}, u32[]{:S(2)}) collective-permute-start(bf16[128,1024]{1,0:T(8,128)(2,1)S(1)} %get-tuple-element.101), channel_id=1, source_target_pairs={{0,2},{1,3},{2,0},{3,1},{4,6},{5,7},{6,4},{7,5},{8,10},{9,11},{10,... | collective-permute-start | bytes 786440 | tf_op jit(solution)/shard_map/ppermute | solution.py:26
  28.3 0.7 copy-start.1
  30.2 5.9 %collective-permute-start.17 = (f32[1,256]{1,0:T(1,128)S(1)}, f32[1,256]{1,0:T(1,128)S(1)}, u32[]{:S(2)}, u32[]{:S(2)}) collective-permute-start(f32[1,256]{1,0:T(1,128)S(1)} %get-tuple-element.98), channel_id=1, source_target_pairs={{0,96},{1,97},{2,98},{3,99},{4,100},{5,101},{6,102},{7,103},{8,104... | collective-permute-start | bytes 3080 | tf_op jit(solution)/shard_map/ppermute | solution.py:26
  33.2 5.1 %collective-permute-start.18 = (f32[1,256]{1,0:T(1,128)S(1)}, f32[1,256]{1,0:T(1,128)S(1)}, u32[]{:S(2)}, u32[]{:S(2)}) collective-permute-start(f32[1,256]{1,0:T(1,128)S(1)} %get-tuple-element.98), channel_id=1, source_target_pairs={{0,64},{1,65},{2,66},{3,67},{4,68},{5,69},{6,70},{7,71},{8,72},{9,... | collective-permute-start | bytes 3080 | tf_op jit(solution)/shard_map/ppermute | solution.py:26
  33.2 5.1 %collective-permute-start.19 = (f32[1,256]{1,0:T(1,128)S(1)}, f32[1,256]{1,0:T(1,128)S(1)}, u32[]{:S(2)}, u32[]{:S(2)}) collective-permute-start(f32[1,256]{1,0:T(1,128)S(1)} %get-tuple-element.98), channel_id=1, source_target_pairs={{0,32},{1,33},{2,34},{3,35},{4,36},{5,37},{6,38},{7,39},{8,40},{9,... | collective-permute-start | bytes 3080 | tf_op jit(solution)/shard_map/ppermute | solution.py:26
  38.4 6.3 %collective-permute-start.24 = (bf16[256,1024]{1,0:T(8,128)(2,1)S(1)}, bf16[256,1024]{1,0:T(8,128)(2,1)S(1)}, u32[]{:S(2)}, u32[]{:S(2)}) collective-permute-start(bf16[256,1024]{1,0:T(8,128)(2,1)S(1)} %collective-permute-done.14.refs_0_.refs_18_), channel_id=1, source_target_pairs={{0,2},{1,3},{2,0},{3,1},{4,6},{5,7},{6,4},{7,5},{8,10},{9,11},{10,... | collective-permute-start | bytes 1572872 | tf_op jit(solution)/shard_map/ppermute | solution.py:26
  38.4 7.4 %collective-permute-start.25 = (bf16[256,1024]{1,0:T(8,128)(2,1)S(1)}, bf16[256,1024]{1,0:T(8,128)(2,1)S(1)}, u32[]{:S(2)}, u32[]{:S(2)}) collective-permute-start(bf16[256,1024]{1,0:T(8,128)(2,1)S(1)} %collective-permute-done.15.refs_0_.refs_20_), channel_id=1, source_target_pairs={{0,2},{1,3},{2,0},{3,1},{4,6},{5,7},{6,4},{7,5},{8,10},{9,11},{10,... | collective-permute-start | bytes 1572872 | tf_op jit(solution)/shard_map/ppermute | solution.py:26
  39.0 9.6 %collective-permute-start.22 = (bf16[128,1024]{1,0:T(8,128)(2,1)S(1)}, bf16[128,1024]{1,0:T(8,128)(2,1)S(1)}, u32[]{:S(2)}, u32[]{:S(2)}) collective-permute-start(bf16[128,1024]{1,0:T(8,128)(2,1)S(1)} %slice.46), channel_id=1, source_target_pairs={{0,12},{1,13},{2,14},{3,15},{4,8},{5,9},{6,10},{7,11},{8,4},{9,5},... | collective-permute-start | bytes 786440 | tf_op jit(solution)/shard_map/ppermute | solution.py:26
  41.1 7.9 %collective-permute-start.23 = (bf16[128,1024]{1,0:T(8,128)(2,1)S(1)}, bf16[128,1024]{1,0:T(8,128)(2,1)S(1)}, u32[]{:S(2)}, u32[]{:S(2)}) collective-permute-start(bf16[128,1024]{1,0:T(8,128)(2,1)S(1)} %slice.47), channel_id=1, source_target_pairs={{0,4},{1,5},{2,6},{3,7},{4,0},{5,1},{6,2},{7,3},{8,12},{9,13},{10,... | collective-permute-start | bytes 786440 | tf_op jit(solution)/shard_map/ppermute | solution.py:26
  41.2 3.6 %collective-permute-start.26 = (f32[1,256]{1,0:T(1,128)S(1)}, f32[1,256]{1,0:T(1,128)S(1)}, u32[]{:S(2)}, u32[]{:S(2)}) collective-permute-start(f32[1,256]{1,0:T(1,128)S(1)} %get-tuple-element.114), channel_id=1, source_target_pairs={{0,16},{1,17},{2,18},{3,19},{4,20},{5,21},{6,22},{7,23},{8,24},{9,... | collective-permute-start | bytes 3080 | tf_op jit(solution)/shard_map/ppermute | solution.py:26
  49.1 1.5 %collective-permute-start.27 = (bf16[128,1024]{1,0:T(8,128)(2,1)S(1)}, bf16[128,1024]{1,0:T(8,128)(2,1)S(1)}, u32[]{:S(2)}, u32[]{:S(2)}) collective-permute-start(bf16[128,1024]{1,0:T(8,128)(2,1)S(1)} %collective-permute-done.22.refs_0_.refs_22_), channel_id=1, source_target_pairs={{0,2},{1,3},{2,0},{3,1},{4,6},{5,7},{6,4},{7,5},{8,10},{9,11},{10,... | collective-permute-start | bytes 786440 | tf_op jit(solution)/shard_map/ppermute | solution.py:26
  49.1 1.9 %collective-permute-start.28 = (bf16[128,1024]{1,0:T(8,128)(2,1)S(1)}, bf16[128,1024]{1,0:T(8,128)(2,1)S(1)}, u32[]{:S(2)}, u32[]{:S(2)}) collective-permute-start(bf16[128,1024]{1,0:T(8,128)(2,1)S(1)} %collective-permute-done.23.refs_1_.refs_23_), channel_id=1, source_target_pairs={{0,2},{1,3},{2,0},{3,1},{4,6},{5,7},{6,4},{7,5},{8,10},{9,11},{10,... | collective-permute-start | bytes 786440 | tf_op jit(solution)/shard_map/ppermute | solution.py:26
  51.7 1.3 %collective-permute-start.30 = (f32[2,1024]{1,0:T(2,128)S(1)}, f32[2,1024]{1,0:T(2,128)S(1)}, u32[]{:S(2)}, u32[]{:S(2)}) collective-permute-start(f32[2,1024]{1,0:T(2,128)S(1)} %maximum_maximum_fusion.1), channel_id=1, source_target_pairs={{0,2},{1,3},{2,0},{3,1},{4,6},{5,7},{6,4},{7,5},{8,10},{9,11},{10,... | collective-permute-start | bytes 24584 | tf_op jit(solution)/shard_map/ppermute | solution.py:26
  53.0 3.7 %collective-permute-start.31 = (f32[2,1024]{1,0:T(2,128)S(1)}, f32[2,1024]{1,0:T(2,128)S(1)}, u32[]{:S(2)}, u32[]{:S(2)}) collective-permute-start(f32[2,1024]{1,0:T(2,128)S(1)} %log_add_fusion.2), channel_id=1, source_target_pairs={{0,4},{1,5},{2,6},{3,7},{4,0},{5,1},{6,2},{7,3},{8,12},{9,13},{10,... | collective-permute-start | bytes 24584 | tf_op jit(solution)/shard_map/ppermute | solution.py:26
  53.4 5.2 %collective-permute-start.29 = (f32[2,512]{1,0:T(2,128)S(1)}, f32[2,512]{1,0:T(2,128)S(1)}, u32[]{:S(2)}, u32[]{:S(2)}) collective-permute-start(f32[2,512]{1,0:T(2,128)S(1)} %pad_maximum_fusion.3.sent_ref), channel_id=1, source_target_pairs={{0,1},{1,0},{2,3},{3,2},{4,5},{5,4},{6,7},{7,6},{8,9},{9,8},{10,11... | collective-permute-start | bytes 12296 | tf_op jit(solution)/shard_map/ppermute | solution.py:26
  56.8 4.9 %collective-permute-start.32 = (f32[2,1024]{1,0:T(2,128)S(1)}, f32[2,1024]{1,0:T(2,128)S(1)}, u32[]{:S(2)}, u32[]{:S(2)}) collective-permute-start(f32[2,1024]{1,0:T(2,128)S(1)} %log_add_fusion.1), channel_id=1, source_target_pairs={{0,12},{1,13},{2,14},{3,15},{4,8},{5,9},{6,10},{7,11},{8,4},{9,5},... | collective-permute-start | bytes 24584 | tf_op jit(solution)/shard_map/ppermute | solution.py:26
  63.5 9.8 %collective-permute-start.34 = (bf16[256,512]{1,0:T(8,128)(2,1)S(1)}, bf16[256,512]{1,0:T(8,128)(2,1)S(1)}, u32[]{:S(2)}, u32[]{:S(2)}) collective-permute-start(bf16[256,512]{1,0:T(8,128)(2,1)S(1)} %get-tuple-element.139), channel_id=1, source_target_pairs={{0,1},{1,0},{2,3},{3,2},{4,5},{5,4},{6,7},{7,6},{8,9},{9,8},{10,11... | collective-permute-start | bytes 786440 | tf_op jit(solution)/shard_map/ppermute | solution.py:26
  68.6 8.8 %collective-permute-start.33 = (bf16[256,512]{1,0:T(8,128)(2,1)S(1)}, bf16[256,512]{1,0:T(8,128)(2,1)S(1)}, u32[]{:S(2)}, u32[]{:S(2)}) collective-permute-start(bf16[256,512]{1,0:T(8,128)(2,1)S(1)} %get-tuple-element.137), channel_id=1, source_target_pairs={{0,1},{1,0},{2,3},{3,2},{4,5},{5,4},{6,7},{7,6},{8,9},{9,8},{10,11... | collective-permute-start | bytes 786440 | tf_op jit(solution)/shard_map/ppermute | solution.py:26

commit v2 on v1

--- a/solution.py
+++ b/solution.py
@@ -130,9 +130,18 @@
 
 
 def own_kernel(
-    half_ref, block_ref, sharp_ref, left_ref, right_ref, pos_ref, emb_ref, score_ref, lse_ref, hit_ref
+    half_ref, block_ref, sharp_ref, whole_ref, other_ref, pos_ref,
+    emb_ref, score_ref, lse_ref, hit_ref, left_ref, right_ref, sems,
 ):
     half = half_ref[0]
+    copies = [
+        pltpu.make_async_copy(source, target, sems.at[j])
+        for j, (source, target) in enumerate(((whole_ref, left_ref), (other_ref, right_ref)))
+    ]
+    for copy in copies:
+        copy.start()
+    for copy in copies:
+        copy.wait()
     embed_rows(left_ref, right_ref, emb_ref)
     mine = pl.ds(pl.multiple_of(half * HALF, HALF), HALF)
     score_ref[...] = products(emb_ref[...], emb_ref[mine, :]) * sharp_ref[0]
@@ -268,12 +277,18 @@
     first, *pieces = call(key_kernel, (bf16(HALF, WIDTH), piece, piece), (), by_group(group[0], swap_keys, near_rows, far_rows))
     held = {0: [first], 1: [swap(first, X[1])], 3: [swap(first, X[3])]}
     over, tiled = {0: [swap(piece, CORE) for piece in pieces]}, {}
-    emb, own_scores, own_column, own_hit = call(
+    emb, own_scores, own_column, own_hit, left, right = pl.pallas_call(
         own_kernel,
-        (bf16(ROWS, WIDTH), f32(ROWS, HALF), f32(1, HALF), f32(1, HALF)),
-        (*place, sharp),
-        (projected, other, pos),
-    )
+        out_shape=(
+            bf16(ROWS, WIDTH), f32(ROWS, HALF), f32(1, HALF), f32(1, HALF),
+            bf16(ROWS, WIDTH // 2), bf16(ROWS, WIDTH // 2),
+        ),
+        in_specs=[spec(pltpu.SMEM)] * 3 + [spec(pltpu.HBM), spec(pltpu.HBM), spec()],
+        out_specs=(spec(),) * 6,
+        scratch_shapes=[pltpu.SemaphoreType.DMA((2,))],
+        compiler_params=pltpu.CompilerParams(vmem_limit_bytes=VMEM_BYTES),
+        cost_estimate=pl.CostEstimate(flops=1, bytes_accessed=1, transcendentals=0),
+    )(*place, sharp, projected, other, pos)
     way = group[0] + 1
     met_column = own_column
     for along_y in (1, 2, 3):
@@ -323,7 +338,7 @@
             functools.partial(grad_kernel, start),
             (f32(HALF, WIDTH // 2), bf16(HALF, WIDTH // 2)),
             (*place, sharp),
-            (lse, column, projected, other, pos, own_scores, emb, *[t[0] for t in tiled], *keys),
+            (lse, column, left, right, pos, own_scores, emb, *[t[0] for t in tiled], *keys),
             scratch=[pltpu.VMEM((HALF, 9 * HALF), BF16)],
         )
         near.append(out[0])

time: 79.9 us -> 81.1 us (1.015); the launches traced: 78.6 us -> 80.8 us
  waiting for transfers between devices: 30.9 us -> 34.6 us
  starting transfers between devices: 29.3 us -> 27.7 us
    ppermute x23, waiting for transfers between devices: 30.9 us -> 34.6 us  [swap(): return lax.ppermute(value, ('tour', 'feat'), pairs)]
    ppermute x23, starting transfers between devices: 29.3 us -> 27.7 us  [swap(): return lax.ppermute(value, ('tour', 'feat'), pairs)]
    pallas_call x0 -> x1, Pallas kernels: none -> 1.25 us  [per_device(): pl.pallas_call(own_kernel, out_shape=(bf16(ROWS, WIDTH), f32(ROWS, HALF),...]
    pallas_call x10 -> x9, Pallas kernels: 11.7 us -> 10.6 us  [call(): pl.pallas_call(body, out_shape=out_shape, in_specs=[spec(pltpu.SMEM)] * l...]
  transfers between devices with their start and end apart: 23 -> 23, of which waited for: 14 -> 12; matrix products, arithmetic and copies ran while one was open for 0% -> 0% of each run, Pallas kernels for 14% -> 14%
where the time goes in v2:
time: 81.1 us; the launch traced here: 80.8 us
  waiting for transfers between devices  34.6 us (43%)
  starting transfers between devices  27.7 us (34%)
  Pallas kernels  13.5 us (17%)
  between operations  2.78 us (3%)
  other arithmetic  1.44 us (2%)
    ppermute x23, waiting for transfers between devices, swap(): return lax.ppermute(value, ('tour', 'feat'), pairs)  34.6 us
    ppermute x23, starting transfers between devices, swap(): return lax.ppermute(value, ('tour', 'feat'), pairs)  27.7 us
    pallas_call x9, Pallas kernels, call(): pl.pallas_call(body, out_shape=out_shape, in_specs=[spec(pltpu.SMEM)] * l...  10.6 us
    pallas_call x1, Pallas kernels, per_device(): pl.pallas_call(prep_kernel, out_shape=(jax.ShapeDtypeStruct((1,), jnp.int...  1.64 us
  transfers between devices with their start and end apart: 23, of which 12 were waited for; matrix products, arithmetic and copies ran while one was open for 0% of the time, Pallas kernels for 14%

profile of v2, /device:TPU:0, one launch (start us, length us, event | category | flops | bytes accessed | tf_op | source)
XLA Modules:
  0.0 80.8 jit_solution(8058950662249567055)
XLA Ops:
  0.6 4.0 %collective-permute-start.16 = (bf16[512,512]{1,0:T(8,128)(2,1)}, bf16[512,512]{1,0:T(8,128)(2,1)S(1)}, u32[]{:S(2)}, u32[]{:S(2)}) collective-permute-start(bf16[512,512]{1,0:T(8,128)(2,1)} %whole_ref.3), channel_id=1, source_target_pairs={{0,1},{1,0},{2,3},{3,2},{4,5},{5,4},{6,7},{7,6},{8,9},{9,8},{10,11... | collective-permute-start | bytes 1572872 | tf_op jit(solution)/shard_map/ppermute | solution.py:26
  4.7 1.6 %shard_map.59 = (s32[1]{0:T(128)}, bf16[256,512]{1,0:T(8,128)(2,1)S(1)}, bf16[256,512]{1,0:T(8,128)(2,1)S(1)}) custom-call(s32[1]{0:T(128)} %bitcast.half_ref.refs_0_, s32[8,64]{1,0:T(8,128)} %partner_ref.1, bf16[512,512]{1,0:T(8,128)(2,1)} %whole_ref.3), custom_call_target="tpu_custom_call" | custom-call | tf_op jit(solution)/shard_map/pallas_call | solution.py:269
  7.0 17.7 %conditional.1 = (bf16[256,512]{1,0:T(8,128)(2,1)}, bf16[256,512]{1,0:T(8,128)(2,1)}) conditional(s32[]{:T(128)} %bitcast.1, (bf16[256,512]{1,0:T(8,128)(2,1)S(1)}, bf16[256,512]{1,0:T(8,128)(2,1)S(1)}) %tuple.38, (bf16[256,512]{1,0:T(8,128)(2,1)S(1)}, bf16[256,512]{1,0:T(8,128)(2,1)S(1)}) %tuple.38, ...), branch_computations={%region_0.0_spmd, %region_1.0_spmd, %region_2.0_spmd, %region_3.0_... | conditional | bytes 2097248 | solution.py:246
  7.0 2.1 %collective-permute-start.4 = (bf16[256,512]{1,0:T(8,128)(2,1)S(1)}, bf16[256,512]{1,0:T(8,128)(2,1)}, u32[]{:S(2)}, u32[]{:S(2)}) collective-permute-start(bf16[256,512]{1,0:T(8,128)(2,1)S(1)} %get-tuple-element.32), channel_id=1, source_target_pairs={{0,48},{1,49},{2,50},{3,51},{4,52},{5,53},{6,54},{7,55},{8,56},{9,... | collective-permute-start | bytes 786440 | tf_op jit(solution)/shard_map/cond/branch_2_fun/ppermute | solution.py:26
  9.1 0.0 collective-permute-start.5
  9.1 8.2 %collective-permute-done.4 = bf16[256,512]{1,0:T(8,128)(2,1)} collective-permute-done((bf16[256,512]{1,0:T(8,128)(2,1)S(1)}, bf16[256,512]{1,0:T(8,128)(2,1)}, u32[]{:S(2)}, u32[]{:S(2)}) %collective-permute-start.4) | collective-permute-done | bytes 262176 | tf_op jit(solution)/shard_map/cond/branch_2_fun/ppermute | solution.py:26
  17.3 7.4 %collective-permute-done.5 = bf16[256,512]{1,0:T(8,128)(2,1)} collective-permute-done((bf16[256,512]{1,0:T(8,128)(2,1)S(1)}, bf16[256,512]{1,0:T(8,128)(2,1)}, u32[]{:S(2)}, u32[]{:S(2)}) %collective-permute-start.5) | collective-permute-done | bytes 262176 | tf_op jit(solution)/shard_map/cond/branch_2_fun/ppermute | solution.py:26
  24.7 1.9 %shard_map.60 = (bf16[256,1024]{1,0:T(8,128)(2,1)S(1)}, bf16[128,1024]{1,0:T(8,128)(2,1)}, bf16[128,1024]{1,0:T(8,128)(2,1)S(1)}) custom-call(bf16[256,512]{1,0:T(8,128)(2,1)} %get-tuple-element.97.left_ref, bf16[256,512]{1,0:T(8,128)(2,1)} %get-tuple-element.98.right_ref), custom_call_target="tpu_custom_call" | custom-call | flops 1 | bytes 1 | tf_op jit(solution)/shard_map/pallas_call | solution.py:34
  26.6 1.5 %collective-permute-start.14 = (bf16[256,1024]{1,0:T(8,128)(2,1)S(1)}, bf16[256,1024]{1,0:T(8,128)(2,1)S(1)}, u32[]{:S(2)}, u32[]{:S(2)}) collective-permute-start(bf16[256,1024]{1,0:T(8,128)(2,1)S(1)} %get-tuple-element.99.refs_0_.refs_15_), channel_id=1, source_target_pairs={{0,4},{1,5},{2,6},{3,7},{4,0},{5,1},{6,2},{7,3},{8,12},{9,13},{10,... | collective-permute-start | bytes 1572872 | tf_op jit(solution)/shard_map/ppermute | solution.py:26
  28.1 2.1 %collective-permute-start.15 = (bf16[256,1024]{1,0:T(8,128)(2,1)S(1)}, bf16[256,1024]{1,0:T(8,128)(2,1)S(1)}, u32[]{:S(2)}, u32[]{:S(2)}) collective-permute-start(bf16[256,1024]{1,0:T(8,128)(2,1)S(1)} %get-tuple-element.99.refs_0_.refs_15_), channel_id=1, source_target_pairs={{0,12},{1,13},{2,14},{3,15},{4,8},{5,9},{6,10},{7,11},{8,4},{9,5},... | collective-permute-start | bytes 1572872 | tf_op jit(solution)/shard_map/ppermute | solution.py:26
  30.2 0.0 collective-permute-start.20
  30.2 0.5 collective-permute-start.21
  31.3 0.0 collective-permute-done.16.other_ref
  31.3 0.0 copy-start.1
  31.4 0.7 copy-done.1
  32.0 1.2 %shard_map.61 = (bf16[512,1024]{1,0:T(8,128)(2,1)S(1)}, f32[512,256]{1,0:T(8,128)S(1)}, f32[1,256]{1,0:T(1,128)S(1)}, f32[1,256]{1,0:T(1,128)S(1)}, bf16[512,512...) custom-call(s32[1]{0:T(128)} %bitcast.half_ref.refs_0_, s32[1]{0:T(128)} %bitcast.3.block_ref.refs_1_, ...), custom_call_target="tpu_custom_call" | custom-call | flops 1 | bytes 1 | tf_op jit(solution)/shard_map/pallas_call | solution.py:280
  33.3 2.7 %collective-permute-start.17 = (f32[1,256]{1,0:T(1,128)S(1)}, f32[1,256]{1,0:T(1,128)S(1)}, u32[]{:S(2)}, u32[]{:S(2)}) collective-permute-start(f32[1,256]{1,0:T(1,128)S(1)} %get-tuple-element.100), channel_id=1, source_target_pairs={{0,96},{1,97},{2,98},{3,99},{4,100},{5,101},{6,102},{7,103},{8,104... | collective-permute-start | bytes 3080 | tf_op jit(solution)/shard_map/ppermute | solution.py:26
  36.0 0.0 collective-permute-done.20.refs_1_.refs_16_
  36.0 0.6 collective-permute-start.18
  36.6 0.0 collective-permute-done.21.refs_2_.refs_17_
  36.6 0.8 %collective-permute-start.19 = (f32[1,256]{1,0:T(1,128)S(1)}, f32[1,256]{1,0:T(1,128)S(1)}, u32[]{:S(2)}, u32[]{:S(2)}) collective-permute-start(f32[1,256]{1,0:T(1,128)S(1)} %get-tuple-element.100), channel_id=1, source_target_pairs={{0,32},{1,33},{2,34},{3,35},{4,36},{5,37},{6,38},{7,39},{8,40},{9,... | collective-permute-start | bytes 3080 | tf_op jit(solution)/shard_map/ppermute | solution.py:26
  38.1 1.1 %shard_map.62 = (f32[2,512,256]{2,1,0:T(8,128)S(1)}, f32[1,512]{1,0:T(1,128)S(1)}, f32[2,256]{1,0:T(2,128)S(1)}) custom-call(f32[1]{0:T(128)} %bitcast.11.sharp_ref, bf16[512,1024]{1,0:T(8,128)(2,1)S(1)} %get-tuple-element.101.emb_ref.refs_9_, bf16[256,1024]{1,0:T(8,128)(2,1)S(1)} %get-tuple-element.99.refs_0_.refs_15_, ...), custom_call_target="tpu_custom_call" | custom-call | flops 1 | bytes 1 | tf_op jit(solution)/shard_map/pallas_call | solution.py:34
  39.2 0.0 collective-permute-done.17
  39.2 1.9 %collective-permute-done.18 = f32[1,256]{1,0:T(1,128)S(1)} collective-permute-done((f32[1,256]{1,0:T(1,128)S(1)}, f32[1,256]{1,0:T(1,128)S(1)}, u32[]{:S(2)}, u32[]{:S(2)}) %collective-permute-start.18) | collective-permute-done | bytes 1056 | tf_op jit(solution)/shard_map/ppermute | solution.py:26
  41.1 0.0 collective-permute-done.19
  41.1 0.0 collective-permute-done.14.refs_0_.refs_18_
  41.1 0.0 collective-permute-done.15.refs_0_.refs_20_
  41.1 0.1 collective-permute-start.24
  41.2 0.5 collective-permute-start.25
  41.8 1.3 %collective-permute-start.22 = (bf16[128,1024]{1,0:T(8,128)(2,1)S(1)}, bf16[128,1024]{1,0:T(8,128)(2,1)S(1)}, u32[]{:S(2)}, u32[]{:S(2)}) collective-permute-start(bf16[128,1024]{1,0:T(8,128)(2,1)S(1)} %slice.46), channel_id=1, source_target_pairs={{0,12},{1,13},{2,14},{3,15},{4,8},{5,9},{6,10},{7,11},{8,4},{9,5},... | collective-permute-start | bytes 786440 | tf_op jit(solution)/shard_map/ppermute | solution.py:26
  43.1 0.0 collective-permute-start.23
  43.1 1.7 %collective-permute-start.26 = (f32[1,256]{1,0:T(1,128)S(1)}, f32[1,256]{1,0:T(1,128)S(1)}, u32[]{:S(2)}, u32[]{:S(2)}) collective-permute-start(f32[1,256]{1,0:T(1,128)S(1)} %get-tuple-element.116), channel_id=1, source_target_pairs={{0,16},{1,17},{2,18},{3,19},{4,20},{5,21},{6,22},{7,23},{8,24},{9,... | collective-permute-start | bytes 3080 | tf_op jit(solution)/shard_map/ppermute | solution.py:26
  44.8 1.8 %collective-permute-done.26 = f32[1,256]{1,0:T(1,128)S(1)} collective-permute-done((f32[1,256]{1,0:T(1,128)S(1)}, f32[1,256]{1,0:T(1,128)S(1)}, u32[]{:S(2)}, u32[]{:S(2)}) %collective-permute-start.26) | collective-permute-done | bytes 1056 | tf_op jit(solution)/shard_map/ppermute | solution.py:26
  46.7 0.0 collective-permute-done.24.refs_1_.refs_19_
  46.7 1.1 %shard_map.63 = (f32[2,512,256]{2,1,0:T(8,128)S(1)}, f32[1,512]{1,0:T(1,128)S(1)}, f32[2,256]{1,0:T(2,128)S(1)}) custom-call(f32[1]{0:T(128)} %bitcast.12.sharp_ref, bf16[512,1024]{1,0:T(8,128)(2,1)S(1)} %get-tuple-element.101.emb_ref.refs_9_, bf16[256,1024]{1,0:T(8,128)(2,1)S(1)} %collective-permute-done.14.refs_0_.refs_18_, ...), custom_call_target="tpu_custom_call" | custom-call | flops 1 | bytes 1 | tf_op jit(solution)/shard_map/pallas_call | solution.py:34
  47.8 0.0 collective-permute-done.25.refs_1_.refs_21_
  47.8 1.1 %shard_map.64 = (f32[2,512,256]{2,1,0:T(8,128)S(1)}, f32[1,512]{1,0:T(1,128)S(1)}, f32[2,256]{1,0:T(2,128)S(1)}) custom-call(f32[1]{0:T(128)} %bitcast.13.sharp_ref, bf16[512,1024]{1,0:T(8,128)(2,1)S(1)} %get-tuple-element.101.emb_ref.refs_9_, bf16[256,1024]{1,0:T(8,128)(2,1)S(1)} %collective-permute-done.15.refs_0_.refs_20_, ...), custom_call_target="tpu_custom_call" | custom-call | flops 1 | bytes 1 | tf_op jit(solution)/shard_map/pallas_call | solution.py:34
  48.9 2.5 %collective-permute-done.22.refs_0_.refs_22_ = bf16[128,1024]{1,0:T(8,128)(2,1)S(1)} collective-permute-done((bf16[128,1024]{1,0:T(8,128)(2,1)S(1)}, bf16[128,1024]{1,0:T(8,128)(2,1)S(1)}, u32[]{:S(2)}, u32[]{:S(2)}) %collective-permute-start.22) | collective-permute-done | bytes 262176 | tf_op jit(solution)/shard_map/ppermute | solution.py:26
  51.4 0.0 collective-permute-done.23.refs_1_.refs_23_
  51.4 0.0 collective-permute-start.27
  51.4 0.5 collective-permute-start.28
  51.9 0.7 shard_map.65
  52.6 0.3 collective-permute-done.27.refs_0_.refs_24_
  52.9 0.4 collective-permute-done.28.refs_1_.refs_25_
  53.3 0.7 shard_map.66
  54.0 0.2 collective-permute-start.30
  54.2 0.1 compare_select_fusion.1
  54.3 1.0 %collective-permute-done.30 = f32[2,1024]{1,0:T(2,128)S(1)} collective-permute-done((f32[2,1024]{1,0:T(2,128)S(1)}, f32[2,1024]{1,0:T(2,128)S(1)}, u32[]{:S(2)}, u32[]{:S(2)}) %collective-permute-start.30) | collective-permute-done | bytes 8224 | tf_op jit(solution)/shard_map/ppermute | solution.py:26
  55.3 0.1 collective-permute-start.31
  55.4 3.3 %collective-permute-start.29 = (f32[2,512]{1,0:T(2,128)S(1)}, f32[2,512]{1,0:T(2,128)S(1)}, u32[]{:S(2)}, u32[]{:S(2)}) collective-permute-start(f32[2,512]{1,0:T(2,128)S(1)} %pad_maximum_fusion.3.sent_ref), channel_id=1, source_target_pairs={{0,1},{1,0},{2,3},{3,2},{4,5},{5,4},{6,7},{7,6},{8,9},{9,8},{10,11... | collective-permute-start | bytes 12296 | tf_op jit(solution)/shard_map/ppermute | solution.py:26
  58.7 0.3 collective-permute-done.31
  59.0 0.1 log_add_fusion.1
  59.1 1.8 %collective-permute-start.32 = (f32[2,1024]{1,0:T(2,128)S(1)}, f32[2,1024]{1,0:T(2,128)S(1)}, u32[]{:S(2)}, u32[]{:S(2)}) collective-permute-start(f32[2,1024]{1,0:T(2,128)S(1)} %log_add_fusion.1), channel_id=1, source_target_pairs={{0,12},{1,13},{2,14},{3,15},{4,8},{5,9},{6,10},{7,11},{8,4},{9,5},... | collective-permute-start | bytes 24584 | tf_op jit(solution)/shard_map/ppermute | solution.py:26
  60.9 0.6 shard_map.67
  61.5 2.5 %collective-permute-done.32 = f32[2,1024]{1,0:T(2,128)S(1)} collective-permute-done((f32[2,1024]{1,0:T(2,128)S(1)}, f32[2,1024]{1,0:T(2,128)S(1)}, u32[]{:S(2)}, u32[]{:S(2)}) %collective-permute-start.32) | collective-permute-done | bytes 8224 | tf_op jit(solution)/shard_map/ppermute | solution.py:26
  64.1 1.7 %shard_map.69 = (f32[256,512]{1,0:T(8,128)S(1)}, bf16[256,512]{1,0:T(8,128)(2,1)S(1)}) custom-call(s32[1]{0:T(128)} %bitcast.half_ref.refs_0_, s32[1]{0:T(128)} %bitcast.3.block_ref.refs_1_, f32[1]{0:T(128)} %bitcast.17.refs_2_, f32[1,512]{1,0:T(1,128)S(1)} %get-tuple-element.125.refs_3_, f32[2,1024]{1,0:T(2,128)S(1)} %log_add_fusion.refs_4_, ...), custom_call_target="tpu_custom_call" | custom-call | flops 1 | bytes 1 | tf_op jit(solution)/shard_map/pallas_call | solution.py:34
  65.8 3.3 %collective-permute-start.34 = (bf16[256,512]{1,0:T(8,128)(2,1)S(1)}, bf16[256,512]{1,0:T(8,128)(2,1)S(1)}, u32[]{:S(2)}, u32[]{:S(2)}) collective-permute-start(bf16[256,512]{1,0:T(8,128)(2,1)S(1)} %get-tuple-element.143), channel_id=1, source_target_pairs={{0,1},{1,0},{2,3},{3,2},{4,5},{5,4},{6,7},{7,6},{8,9},{9,8},{10,11... | collective-permute-start | bytes 786440 | tf_op jit(solution)/shard_map/ppermute | solution.py:26
  69.1 1.7 %shard_map.68 = (f32[256,512]{1,0:T(8,128)S(1)}, bf16[256,512]{1,0:T(8,128)(2,1)S(1)}) custom-call(s32[1]{0:T(128)} %bitcast.half_ref.refs_0_, s32[1]{0:T(128)} %bitcast.3.block_ref.refs_1_, f32[1]{0:T(128)} %bitcast.16.refs_2_, f32[1,512]{1,0:T(1,128)S(1)} %get-tuple-element.125.refs_3_, f32[2,1024]{1,0:T(2,128)S(1)} %log_add_fusion.refs_4_, ...), custom_call_target="tpu_custom_call" | custom-call | flops 1 | bytes 1 | tf_op jit(solution)/shard_map/pallas_call | solution.py:34
  70.9 0.4 collective-permute-start.33
  71.2 4.3 %collective-permute-done.34 = bf16[256,512]{1,0:T(8,128)(2,1)S(1)} collective-permute-done((bf16[256,512]{1,0:T(8,128)(2,1)S(1)}, bf16[256,512]{1,0:T(8,128)(2,1)S(1)}, u32[]{:S(2)}, u32[]{:S(2)}) %collective-permute-start.34) | collective-permute-done | bytes 262176 | tf_op jit(solution)/shard_map/ppermute | solution.py:26
  75.6 0.1 convert_add_fusion
  75.6 4.0 %collective-permute-done.33 = bf16[256,512]{1,0:T(8,128)(2,1)S(1)} collective-permute-done((bf16[256,512]{1,0:T(8,128)(2,1)S(1)}, bf16[256,512]{1,0:T(8,128)(2,1)S(1)}, u32[]{:S(2)}, u32[]{:S(2)}) %collective-permute-start.33) | collective-permute-done | bytes 262176 | tf_op jit(solution)/shard_map/ppermute | solution.py:26
  79.7 0.1 convert_add_fusion.1
  79.8 1.0 %pad_maximum_fusion = f32[512,512]{1,0:T(8,128)} fusion(f32[256,512]{1,0:T(8,128)S(1)} %convert_add_fusion, f32[256,512]{1,0:T(8,128)S(1)} %convert_add_fusion.1), kind=kLoop, calls=%fused_computation | loop fusion | flops 262144 | bytes 2097152 | tf_op jit(solution)/shard_map/concatenate | solution.py:346
  (17 shorter events, 0.2 us)
Async XLA Ops:
  0.6 30.7 %collective-permute-start.16 = (bf16[512,512]{1,0:T(8,128)(2,1)}, bf16[512,512]{1,0:T(8,128)(2,1)S(1)}, u32[]{:S(2)}, u32[]{:S(2)}) collective-permute-start(bf16[512,512]{1,0:T(8,128)(2,1)} %whole_ref.3), channel_id=1, source_target_pairs={{0,1},{1,0},{2,3},{3,2},{4,5},{5,4},{6,7},{7,6},{8,9},{9,8},{10,11... | collective-permute-start | bytes 1572872 | tf_op jit(solution)/shard_map/ppermute | solution.py:26
  4.7 26.7 %copy-start = (bf16[512,512]{1,0:T(8,128)(2,1)S(1)}, bf16[512,512]{1,0:T(8,128)(2,1)}, u32[]{:S(2)}) copy-start(bf16[512,512]{1,0:T(8,128)(2,1)} %whole_ref.3) | copy-start | bytes 1572868
  7.0 10.3 %collective-permute-start.4 = (bf16[256,512]{1,0:T(8,128)(2,1)S(1)}, bf16[256,512]{1,0:T(8,128)(2,1)}, u32[]{:S(2)}, u32[]{:S(2)}) collective-permute-start(bf16[256,512]{1,0:T(8,128)(2,1)S(1)} %get-tuple-element.32), channel_id=1, source_target_pairs={{0,48},{1,49},{2,50},{3,51},{4,52},{5,53},{6,54},{7,55},{8,56},{9,... | collective-permute-start | bytes 786440 | tf_op jit(solution)/shard_map/cond/branch_2_fun/ppermute | solution.py:26
  9.1 15.6 %collective-permute-start.5 = (bf16[256,512]{1,0:T(8,128)(2,1)S(1)}, bf16[256,512]{1,0:T(8,128)(2,1)}, u32[]{:S(2)}, u32[]{:S(2)}) collective-permute-start(bf16[256,512]{1,0:T(8,128)(2,1)S(1)} %get-tuple-element.33), channel_id=1, source_target_pairs={{0,49},{1,48},{2,51},{3,50},{4,53},{5,52},{6,55},{7,54},{8,57},{9,... | collective-permute-start | bytes 786440 | tf_op jit(solution)/shard_map/cond/branch_2_fun/ppermute | solution.py:26
  26.6 14.5 %collective-permute-start.14 = (bf16[256,1024]{1,0:T(8,128)(2,1)S(1)}, bf16[256,1024]{1,0:T(8,128)(2,1)S(1)}, u32[]{:S(2)}, u32[]{:S(2)}) collective-permute-start(bf16[256,1024]{1,0:T(8,128)(2,1)S(1)} %get-tuple-element.99.refs_0_.refs_15_), channel_id=1, source_target_pairs={{0,4},{1,5},{2,6},{3,7},{4,0},{5,1},{6,2},{7,3},{8,12},{9,13},{10,... | collective-permute-start | bytes 1572872 | tf_op jit(solution)/shard_map/ppermute | solution.py:26
  28.1 13.0 %collective-permute-start.15 = (bf16[256,1024]{1,0:T(8,128)(2,1)S(1)}, bf16[256,1024]{1,0:T(8,128)(2,1)S(1)}, u32[]{:S(2)}, u32[]{:S(2)}) collective-permute-start(bf16[256,1024]{1,0:T(8,128)(2,1)S(1)} %get-tuple-element.99.refs_0_.refs_15_), channel_id=1, source_target_pairs={{0,12},{1,13},{2,14},{3,15},{4,8},{5,9},{6,10},{7,11},{8,4},{9,5},... | collective-permute-start | bytes 1572872 | tf_op jit(solution)/shard_map/ppermute | solution.py:26
  30.2 5.8 %collective-permute-start.20 = (bf16[128,1024]{1,0:T(8,128)(2,1)}, bf16[128,1024]{1,0:T(8,128)(2,1)S(1)}, u32[]{:S(2)}, u32[]{:S(2)}) collective-permute-start(bf16[128,1024]{1,0:T(8,128)(2,1)} %get-tuple-element.102), channel_id=1, source_target_pairs={{0,2},{1,3},{2,0},{3,1},{4,6},{5,7},{6,4},{7,5},{8,10},{9,11},{10,... | collective-permute-start | bytes 786440 | tf_op jit(solution)/shard_map/ppermute | solution.py:26
  30.2 6.5 %collective-permute-start.21 = (bf16[128,1024]{1,0:T(8,128)(2,1)S(1)}, bf16[128,1024]{1,0:T(8,128)(2,1)S(1)}, u32[]{:S(2)}, u32[]{:S(2)}) collective-permute-start(bf16[128,1024]{1,0:T(8,128)(2,1)S(1)} %get-tuple-element.103), channel_id=1, source_target_pairs={{0,2},{1,3},{2,0},{3,1},{4,6},{5,7},{6,4},{7,5},{8,10},{9,11},{10,... | collective-permute-start | bytes 786440 | tf_op jit(solution)/shard_map/ppermute | solution.py:26
  31.3 0.7 copy-start.1
  33.3 5.9 %collective-permute-start.17 = (f32[1,256]{1,0:T(1,128)S(1)}, f32[1,256]{1,0:T(1,128)S(1)}, u32[]{:S(2)}, u32[]{:S(2)}) collective-permute-start(f32[1,256]{1,0:T(1,128)S(1)} %get-tuple-element.100), channel_id=1, source_target_pairs={{0,96},{1,97},{2,98},{3,99},{4,100},{5,101},{6,102},{7,103},{8,104... | collective-permute-start | bytes 3080 | tf_op jit(solution)/shard_map/ppermute | solution.py:26
  36.0 5.1 %collective-permute-start.18 = (f32[1,256]{1,0:T(1,128)S(1)}, f32[1,256]{1,0:T(1,128)S(1)}, u32[]{:S(2)}, u32[]{:S(2)}) collective-permute-start(f32[1,256]{1,0:T(1,128)S(1)} %get-tuple-element.100), channel_id=1, source_target_pairs={{0,64},{1,65},{2,66},{3,67},{4,68},{5,69},{6,70},{7,71},{8,72},{9,... | collective-permute-start | bytes 3080 | tf_op jit(solution)/shard_map/ppermute | solution.py:26
  36.6 4.4 %collective-permute-start.19 = (f32[1,256]{1,0:T(1,128)S(1)}, f32[1,256]{1,0:T(1,128)S(1)}, u32[]{:S(2)}, u32[]{:S(2)}) collective-permute-start(f32[1,256]{1,0:T(1,128)S(1)} %get-tuple-element.100), channel_id=1, source_target_pairs={{0,32},{1,33},{2,34},{3,35},{4,36},{5,37},{6,38},{7,39},{8,40},{9,... | collective-permute-start | bytes 3080 | tf_op jit(solution)/shard_map/ppermute | solution.py:26
  41.1 5.6 %collective-permute-start.24 = (bf16[256,1024]{1,0:T(8,128)(2,1)S(1)}, bf16[256,1024]{1,0:T(8,128)(2,1)S(1)}, u32[]{:S(2)}, u32[]{:S(2)}) collective-permute-start(bf16[256,1024]{1,0:T(8,128)(2,1)S(1)} %collective-permute-done.14.refs_0_.refs_18_), channel_id=1, source_target_pairs={{0,2},{1,3},{2,0},{3,1},{4,6},{5,7},{6,4},{7,5},{8,10},{9,11},{10,... | collective-permute-start | bytes 1572872 | tf_op jit(solution)/shard_map/ppermute | solution.py:26
  41.2 6.6 %collective-permute-start.25 = (bf16[256,1024]{1,0:T(8,128)(2,1)S(1)}, bf16[256,1024]{1,0:T(8,128)(2,1)S(1)}, u32[]{:S(2)}, u32[]{:S(2)}) collective-permute-start(bf16[256,1024]{1,0:T(8,128)(2,1)S(1)} %collective-permute-done.15.refs_0_.refs_20_), channel_id=1, source_target_pairs={{0,2},{1,3},{2,0},{3,1},{4,6},{5,7},{6,4},{7,5},{8,10},{9,11},{10,... | collective-permute-start | bytes 1572872 | tf_op jit(solution)/shard_map/ppermute | solution.py:26
  41.8 9.6 %collective-permute-start.22 = (bf16[128,1024]{1,0:T(8,128)(2,1)S(1)}, bf16[128,1024]{1,0:T(8,128)(2,1)S(1)}, u32[]{:S(2)}, u32[]{:S(2)}) collective-permute-start(bf16[128,1024]{1,0:T(8,128)(2,1)S(1)} %slice.46), channel_id=1, source_target_pairs={{0,12},{1,13},{2,14},{3,15},{4,8},{5,9},{6,10},{7,11},{8,4},{9,5},... | collective-permute-start | bytes 786440 | tf_op jit(solution)/shard_map/ppermute | solution.py:26
  43.1 8.3 %collective-permute-start.23 = (bf16[128,1024]{1,0:T(8,128)(2,1)S(1)}, bf16[128,1024]{1,0:T(8,128)(2,1)S(1)}, u32[]{:S(2)}, u32[]{:S(2)}) collective-permute-start(bf16[128,1024]{1,0:T(8,128)(2,1)S(1)} %slice.47), channel_id=1, source_target_pairs={{0,4},{1,5},{2,6},{3,7},{4,0},{5,1},{6,2},{7,3},{8,12},{9,13},{10,... | collective-permute-start | bytes 786440 | tf_op jit(solution)/shard_map/ppermute | solution.py:26
  43.1 3.6 %collective-permute-start.26 = (f32[1,256]{1,0:T(1,128)S(1)}, f32[1,256]{1,0:T(1,128)S(1)}, u32[]{:S(2)}, u32[]{:S(2)}) collective-permute-start(f32[1,256]{1,0:T(1,128)S(1)} %get-tuple-element.116), channel_id=1, source_target_pairs={{0,16},{1,17},{2,18},{3,19},{4,20},{5,21},{6,22},{7,23},{8,24},{9,... | collective-permute-start | bytes 3080 | tf_op jit(solution)/shard_map/ppermute | solution.py:26
  51.4 1.5 %collective-permute-start.27 = (bf16[128,1024]{1,0:T(8,128)(2,1)S(1)}, bf16[128,1024]{1,0:T(8,128)(2,1)S(1)}, u32[]{:S(2)}, u32[]{:S(2)}) collective-permute-start(bf16[128,1024]{1,0:T(8,128)(2,1)S(1)} %collective-permute-done.22.refs_0_.refs_22_), channel_id=1, source_target_pairs={{0,2},{1,3},{2,0},{3,1},{4,6},{5,7},{6,4},{7,5},{8,10},{9,11},{10,... | collective-permute-start | bytes 786440 | tf_op jit(solution)/shard_map/ppermute | solution.py:26
  51.4 1.9 %collective-permute-start.28 = (bf16[128,1024]{1,0:T(8,128)(2,1)S(1)}, bf16[128,1024]{1,0:T(8,128)(2,1)S(1)}, u32[]{:S(2)}, u32[]{:S(2)}) collective-permute-start(bf16[128,1024]{1,0:T(8,128)(2,1)S(1)} %collective-permute-done.23.refs_1_.refs_23_), channel_id=1, source_target_pairs={{0,2},{1,3},{2,0},{3,1},{4,6},{5,7},{6,4},{7,5},{8,10},{9,11},{10,... | collective-permute-start | bytes 786440 | tf_op jit(solution)/shard_map/ppermute | solution.py:26
  54.0 1.3 %collective-permute-start.30 = (f32[2,1024]{1,0:T(2,128)S(1)}, f32[2,1024]{1,0:T(2,128)S(1)}, u32[]{:S(2)}, u32[]{:S(2)}) collective-permute-start(f32[2,1024]{1,0:T(2,128)S(1)} %maximum_maximum_fusion.1), channel_id=1, source_target_pairs={{0,2},{1,3},{2,0},{3,1},{4,6},{5,7},{6,4},{7,5},{8,10},{9,11},{10,... | collective-permute-start | bytes 24584 | tf_op jit(solution)/shard_map/ppermute | solution.py:26
  55.3 3.7 %collective-permute-start.31 = (f32[2,1024]{1,0:T(2,128)S(1)}, f32[2,1024]{1,0:T(2,128)S(1)}, u32[]{:S(2)}, u32[]{:S(2)}) collective-permute-start(f32[2,1024]{1,0:T(2,128)S(1)} %log_add_fusion.2), channel_id=1, source_target_pairs={{0,4},{1,5},{2,6},{3,7},{4,0},{5,1},{6,2},{7,3},{8,12},{9,13},{10,... | collective-permute-start | bytes 24584 | tf_op jit(solution)/shard_map/ppermute | solution.py:26
  55.4 5.5 %collective-permute-start.29 = (f32[2,512]{1,0:T(2,128)S(1)}, f32[2,512]{1,0:T(2,128)S(1)}, u32[]{:S(2)}, u32[]{:S(2)}) collective-permute-start(f32[2,512]{1,0:T(2,128)S(1)} %pad_maximum_fusion.3.sent_ref), channel_id=1, source_target_pairs={{0,1},{1,0},{2,3},{3,2},{4,5},{5,4},{6,7},{7,6},{8,9},{9,8},{10,11... | collective-permute-start | bytes 12296 | tf_op jit(solution)/shard_map/ppermute | solution.py:26
  59.1 4.9 %collective-permute-start.32 = (f32[2,1024]{1,0:T(2,128)S(1)}, f32[2,1024]{1,0:T(2,128)S(1)}, u32[]{:S(2)}, u32[]{:S(2)}) collective-permute-start(f32[2,1024]{1,0:T(2,128)S(1)} %log_add_fusion.1), channel_id=1, source_target_pairs={{0,12},{1,13},{2,14},{3,15},{4,8},{5,9},{6,10},{7,11},{8,4},{9,5},... | collective-permute-start | bytes 24584 | tf_op jit(solution)/shard_map/ppermute | solution.py:26
  65.8 9.7 %collective-permute-start.34 = (bf16[256,512]{1,0:T(8,128)(2,1)S(1)}, bf16[256,512]{1,0:T(8,128)(2,1)S(1)}, u32[]{:S(2)}, u32[]{:S(2)}) collective-permute-start(bf16[256,512]{1,0:T(8,128)(2,1)S(1)} %get-tuple-element.143), channel_id=1, source_target_pairs={{0,1},{1,0},{2,3},{3,2},{4,5},{5,4},{6,7},{7,6},{8,9},{9,8},{10,11... | collective-permute-start | bytes 786440 | tf_op jit(solution)/shard_map/ppermute | solution.py:26
  70.9 8.8 %collective-permute-start.33 = (bf16[256,512]{1,0:T(8,128)(2,1)S(1)}, bf16[256,512]{1,0:T(8,128)(2,1)S(1)}, u32[]{:S(2)}, u32[]{:S(2)}) collective-permute-start(bf16[256,512]{1,0:T(8,128)(2,1)S(1)} %get-tuple-element.141), channel_id=1, source_target_pairs={{0,1},{1,0},{2,3},{3,2},{4,5},{5,4},{6,7},{7,6},{8,9},{9,8},{10,11... | collective-permute-start | bytes 786440 | tf_op jit(solution)/shard_map/ppermute | solution.py:26
